TPU v7x, 32 devices: a whole 2x2x4 slice. The times are simulated.
32 devices in a mesh: groups: 1, seq: 32 (over z, y, x, core).
Axes of the slice: x: 2, y: 2, z: 4, core: 2. Of those that a mesh axis runs over, the one named last changes fastest.
Arguments:
- queries: bfloat16 [32, 8192], P(('groups', 'seq')), may hold values from -15 to 15
- shared_prompt_keys: bfloat16 [65536, 1024], P(('groups', 'seq')), may hold values from -6.1 to 6.1
- shared_prompt_values: bfloat16 [65536, 1024], P(('groups', 'seq')), may hold values from -6 to 6
- private_cached_keys: bfloat16 [32, 256, 1024], P(('groups', 'seq')), may hold values from -9.1 to 9.1
- private_cached_values: bfloat16 [32, 256, 1024], P(('groups', 'seq')), may hold values from -6 to 6
- token_keys: bfloat16 [32, 1024], P(('groups', 'seq')), may hold values from -12 to 12
- token_values: bfloat16 [32, 1024], P(('groups', 'seq')), may hold values from -6 to 6
- suffix_lengths: int32 [32], P(('groups', 'seq')), may hold values from 1 to 256, as said below
- block_prompts: int32 [4], P('groups'), may hold values from 0 to 3, as said below
- out_weight: bfloat16 [8192, 8192], P(None, 'seq'), may hold values from -0.0625 to 0.0625
Outputs:
- projected: bfloat16 [32, 8192], P(('groups', 'seq'))
Inputs may be any that keep to these rules, and one draw needn't show every extreme that they name: `block_prompts`: no prompt is read by more than 2 blocks, and one prompt is read by exactly 2. `suffix_lengths`: some continuation has exactly 256 live slots.
All inputs are finite; a program needn't handle non-finite values.
Results may differ from a plain program's by a relative error of at most 0.0053.
Values may be sent and summed in bfloat16 or wider, within the bound.
A program may use at most 128 MiB of HBM per device.

v0:
```python
import math

import jax
import jax.numpy as jnp
from jax import lax
from jax.sharding import PartitionSpec as P

QUERY_HEADS = 64
KEY_VALUE_HEADS = 8
HEAD_SIZE = 128
PROMPT_COUNT = 4


masked_score = -1e30


def head_scores(operands):
    queries_head, keys_head, values_head = operands
    score_scale = 1.0 / math.sqrt(HEAD_SIZE)
    scores = (
        jnp.einsum("rgd,pd->rgp", queries_head, keys_head, preferred_element_type=jnp.float32)
        * score_scale
    )
    row_max = jnp.max(scores, axis=2)
    weights = jnp.exp(scores - row_max[..., None])
    rows_overall = jnp.sum(weights, axis=2)
    head_part = (
        jnp.einsum(
            "rgp,pd->rgd",
            weights.astype(jnp.bfloat16),
            values_head,
            preferred_element_type=jnp.float32,
        )
        / rows_overall[..., None]
    )
    return (row_max, rows_overall, head_part.astype(jnp.bfloat16))


def body(
    queries,
    shared_prompt_keys,
    shared_prompt_values,
    private_cached_keys,
    private_cached_values,
    token_keys,
    token_values,
    suffix_lengths,
    block_prompts,
    out_weight,
):
    count_of_rows, model_width = queries.shape
    devices_seq = lax.axis_size("seq")
    query_group_count = QUERY_HEADS // KEY_VALUE_HEADS
    prompt_segment = devices_seq // PROMPT_COUNT
    all_rows = count_of_rows * devices_seq
    rows_in_block = all_rows // PROMPT_COUNT
    blocks = all_rows // rows_in_block
    count_of_slots = min(blocks, (blocks + PROMPT_COUNT - 1) // PROMPT_COUNT + 1)
    my_index = lax.axis_index("seq")
    own_prompt = my_index // prompt_segment
    matches = block_prompts == own_prompt
    slot_rank = jnp.cumsum(matches.astype(jnp.int32)) - 1
    slot_ids = jnp.arange(count_of_slots, dtype=jnp.int32)
    chosen = matches[None, :] & (slot_rank[None, :] == slot_ids[:, None])
    filled = jnp.any(chosen, axis=1)
    block_ids = jnp.arange(blocks, dtype=jnp.int32)
    slot_block = jnp.sum(jnp.where(chosen, block_ids[None, :], 0), axis=1)
    everyone = lax.all_gather(queries, "seq", axis=0, tiled=True)
    selected_items = jnp.take(
        everyone.reshape(blocks, rows_in_block, model_width), slot_block, axis=0
    )
    heads_of_queries = selected_items.reshape(
        count_of_slots * rows_in_block, KEY_VALUE_HEADS, query_group_count, HEAD_SIZE
    ).transpose(1, 0, 2, 3)
    heads_of_keys = shared_prompt_keys.reshape(-1, KEY_VALUE_HEADS, HEAD_SIZE).transpose(1, 0, 2)
    heads_of_values = shared_prompt_values.reshape(-1, KEY_VALUE_HEADS, HEAD_SIZE).transpose(
        1, 0, 2
    )
    head_max, head_total, head_part = lax.map(
        head_scores, (heads_of_queries, heads_of_keys, heads_of_values)
    )
    max_rows = head_max.transpose(1, 0, 2).reshape(count_of_slots, rows_in_block, QUERY_HEADS)
    total_rows = head_total.transpose(1, 0, 2).reshape(count_of_slots, rows_in_block, QUERY_HEADS)
    part_rows = head_part.transpose(1, 0, 2, 3).reshape(count_of_slots, rows_in_block, model_width)
    score_scale = 1.0 / math.sqrt(HEAD_SIZE)
    private_length = private_cached_keys.shape[1]
    continuation_queries = queries.reshape(
        count_of_rows, KEY_VALUE_HEADS, query_group_count, HEAD_SIZE
    )
    cached_key_rows = private_cached_keys.reshape(
        count_of_rows, private_length, KEY_VALUE_HEADS, HEAD_SIZE
    )
    cached_value_rows = private_cached_values.reshape(
        count_of_rows, private_length, KEY_VALUE_HEADS, HEAD_SIZE
    )
    latest_key = token_keys.reshape(count_of_rows, KEY_VALUE_HEADS, HEAD_SIZE)
    latest_value = token_values.reshape(count_of_rows, KEY_VALUE_HEADS, HEAD_SIZE)
    positions = jnp.arange(private_length, dtype=jnp.int32)
    live_keys = positions[None, :] < suffix_lengths[:, None]
    scores = (
        jnp.einsum(
            "rkgd,rskd->rkgs",
            continuation_queries,
            cached_key_rows,
            preferred_element_type=jnp.float32,
        )
        * score_scale
    )
    scores = jnp.where(live_keys[:, None, None, :], scores, masked_score)
    fresh_score = (
        jnp.einsum(
            "rkgd,rkd->rkg", continuation_queries, latest_key, preferred_element_type=jnp.float32
        )
        * score_scale
    )
    suffix_max = jnp.maximum(jnp.max(scores, axis=3), fresh_score)
    weights = jnp.exp(scores - suffix_max[..., None])
    fresh_weight = jnp.exp(fresh_score - suffix_max)
    suffix_total = jnp.sum(weights, axis=3) + fresh_weight
    suffix_sum = jnp.einsum(
        "rkgs,rskd->rkgd",
        weights.astype(jnp.bfloat16),
        cached_value_rows,
        preferred_element_type=jnp.float32,
    )
    fresh_term = (
        fresh_weight.astype(jnp.bfloat16).astype(jnp.float32)[..., None]
        * latest_value.astype(jnp.float32)[:, :, None, :]
    )
    suffix_part = ((suffix_sum + fresh_term) / suffix_total[..., None]).reshape(
        count_of_rows, QUERY_HEADS, HEAD_SIZE
    )
    suffix_max = suffix_max.reshape(count_of_rows, QUERY_HEADS)
    suffix_total = suffix_total.reshape(count_of_rows, QUERY_HEADS)
    target_block = jnp.where(filled, slot_block, blocks)
    send_part = (
        jnp.zeros((blocks, rows_in_block, model_width), jnp.bfloat16)
        .at[target_block]
        .set(part_rows, mode="drop")
    )
    send_max = (
        jnp.full((blocks, rows_in_block, QUERY_HEADS), masked_score, jnp.float32)
        .at[target_block]
        .set(max_rows, mode="drop")
    )
    send_total = (
        jnp.zeros((blocks, rows_in_block, QUERY_HEADS), jnp.float32)
        .at[target_block]
        .set(total_rows, mode="drop")
    )
    got_part, got_max, got_total = (
        lax.all_to_all(
            send_part.reshape(all_rows, model_width).astype(jnp.float32),
            "seq",
            split_axis=0,
            concat_axis=0,
            tiled=True,
        ),
        lax.all_to_all(
            send_max.reshape(all_rows, QUERY_HEADS), "seq", split_axis=0, concat_axis=0, tiled=True
        ),
        lax.all_to_all(
            send_total.reshape(all_rows, QUERY_HEADS),
            "seq",
            split_axis=0,
            concat_axis=0,
            tiled=True,
        ),
    )
    part_from = got_part.reshape(devices_seq, count_of_rows, QUERY_HEADS, HEAD_SIZE)
    max_from = got_max.reshape(devices_seq, count_of_rows, QUERY_HEADS)
    total_from = got_total.reshape(devices_seq, count_of_rows, QUERY_HEADS)
    row_best = jnp.maximum(suffix_max, jnp.max(max_from, axis=0))
    factor = total_from * jnp.exp(max_from - row_best[None])
    own_factor = suffix_total * jnp.exp(suffix_max - row_best)
    numerator = own_factor[..., None] * suffix_part + jnp.sum(factor[..., None] * part_from, axis=0)
    denominator = own_factor + jnp.sum(factor, axis=0)
    attention = (
        (numerator / denominator[..., None])
        .astype(jnp.bfloat16)
        .reshape(count_of_rows, model_width)
    )
    panel = jnp.dot(
        lax.all_gather(attention, "seq", axis=0, tiled=True),
        out_weight,
        preferred_element_type=jnp.float32,
    )
    return lax.all_to_all(
        panel.astype(jnp.bfloat16), "seq", split_axis=0, concat_axis=1, tiled=True
    )


def solution(mesh):
    in_specs = (
        P(("groups", "seq"), None),
        P(("groups", "seq"), None),
        P(("groups", "seq"), None),
        P(("groups", "seq"), None, None),
        P(("groups", "seq"), None, None),
        P(("groups", "seq"), None),
        P(("groups", "seq"), None),
        P(("groups", "seq")),
        P("groups"),
        P(None, "seq"),
    )
    out_specs = P(("groups", "seq"), None)
    return jax.shard_map(body, mesh=mesh, in_specs=in_specs, out_specs=out_specs, check_vma=False)
```

profile of v0, /device:TPU:0, one launch (start us, length us, event | category | flops | bytes accessed | tf_op | source)
XLA Modules:
  0.0 194.9 jit_solution(8798379751377624329)
XLA Ops:
  0.0 0.7 convert_bitcast_fusion.1
  1.2 46.4 %all-gather = bf16[32,1,8192]{2,1,0:T(2,128)(2,1)S(1)} all-gather(bf16[1,1,8192]{2,1,0:T(2,128)(2,1)} %bitcast.135), channel_id=1, replica_groups=mesh['groups'=1,'seq'=32] {'seq'}, dimensions={0}, use_global_device_ids=true | all-gather | bytes 540672 | tf_op jit(solution)/shard_map/all_gather | solution.py:68
  47.6 0.6 copy.80
  48.2 0.6 gather_fusion
  49.0 6.5 %copy.45 = bf16[2048,1024]{0,1:T(8,128)(2,1)} copy(bf16[2048,1024]{1,0:T(8,128)(2,1)} %param.13) | data formatting | bytes 8388608 | tf_op args[1]
  55.5 6.5 %copy.46 = bf16[2048,1024]{0,1:T(8,128)(2,1)} copy(bf16[2048,1024]{1,0:T(8,128)(2,1)} %param.14) | data formatting | bytes 8388608 | tf_op args[2]
  62.1 26.2 %while.14 = (s32[]{:T(128)}, f32[8,16,8]{1,2,0:T(8,128)S(1)}, f32[8,16,8]{1,2,0:T(8,128)S(1)}, bf16[8,16,8,128]{3,2,1,0:T(8,128)(2,1)S(1)}, bf16[8,16,8,128]{3,2...) while((s32[]{:T(128)}, f32[8,16,8]{1,2,0:T(8,128)S(1)}, ...), condition=%wide.region_8.9_spmd, body=%wide.region_5.8_spmd.sunk | while | flops 135823104 | bytes 4298329 | solution.py:79
  62.1 1.4 fusion.46
  63.5 0.3 fusion.47
  63.8 1.4 fusion.48
  65.4 1.4 fusion.46
  66.8 0.3 fusion.47
  67.1 1.4 fusion.48
  68.6 1.4 fusion.46
  70.0 0.3 fusion.47
  70.3 1.4 fusion.48
  71.9 1.4 fusion.46
  73.6 1.4 fusion.48
  75.2 1.4 fusion.46
  76.9 1.4 fusion.48
  78.4 1.4 fusion.46
  80.1 1.4 fusion.48
  81.7 1.4 fusion.46
  83.1 0.3 fusion.47
  83.4 1.4 fusion.48
  85.0 1.4 fusion.46
  86.7 1.4 fusion.48
  88.4 0.6 broadcast_in_dim.89
  89.0 1.3 scatter_fusion
  90.3 2.6 %all-to-all-start = ((f32[32,1,64]{2,1,0:T(1,128)}), f32[32,1,64]{2,1,0:T(1,128)S(1)}, u32[]{:S(2)}, u32[]{:S(2)}) async-start(f32[32,1,64]{2,1,0:T(1,128)} %bitcast.26), calls=%async_computation | async-start | bytes 32768 | tf_op jit(solution)/shard_map/all_to_all | solution.py:159
  93.1 0.6 broadcast_in_dim.99
  93.7 1.3 scatter_fusion.1
  95.0 5.0 %all-to-all-done = f32[32,1,64]{2,1,0:T(1,128)S(1)} async-done(((f32[32,1,64]{2,1,0:T(1,128)}), f32[32,1,64]{2,1,0:T(1,128)S(1)}, u32[]{:S(2)}, u32[]{:S(2)}) %all-to-all-start) | async-done | bytes 8224 | tf_op jit(solution)/shard_map/all_to_all | solution.py:159
  100.1 2.5 %all-to-all-start.1 = ((f32[32,1,64]{2,1,0:T(1,128)}), f32[32,1,64]{2,1,0:T(1,128)S(1)}, u32[]{:S(2)}, u32[]{:S(2)}) async-start(f32[32,1,64]{2,1,0:T(1,128)} %bitcast.32), calls=%async_computation.1 | async-start | bytes 32768 | tf_op jit(solution)/shard_map/all_to_all | solution.py:162
  102.9 0.6 scatter_fusion.2
  103.5 2.3 %reshape.394 = f32[32,1,8192]{2,1,0:T(1,128)} reshape(bf16[4,8,8192]{2,1,0:T(8,128)(2,1)S(1)} %scatter_fusion.2) | data formatting | bytes 1572864 | tf_op jit(solution)/shard_map/convert_element_type | solution.py:153
  105.8 3.9 %all-to-all-done.1 = f32[32,1,64]{2,1,0:T(1,128)S(1)} async-done(((f32[32,1,64]{2,1,0:T(1,128)}), f32[32,1,64]{2,1,0:T(1,128)S(1)}, u32[]{:S(2)}, u32[]{:S(2)}) %all-to-all-start.1) | async-done | bytes 8224 | tf_op jit(solution)/shard_map/all_to_all | solution.py:162
  109.7 2.6 %all-to-all-start.2 = ((f32[32,1,8192]{2,1,0:T(1,128)}), f32[32,1,8192]{2,1,0:T(1,128)S(1)}, u32[]{:S(2)}, u32[]{:S(2)}) async-start(f32[32,1,8192]{2,1,0:T(1,128)} %reshape.394), calls=%async_computation.2 | async-start | bytes 2097152 | tf_op jit(solution)/shard_map/all_to_all | solution.py:152
  113.3 0.3 fusion.37
  114.5 24.0 %all-to-all-done.2 = f32[32,1,8192]{2,1,0:T(1,128)S(1)} async-done(((f32[32,1,8192]{2,1,0:T(1,128)}), f32[32,1,8192]{2,1,0:T(1,128)S(1)}, u32[]{:S(2)}, u32[]{:S(2)}) %all-to-all-start.2) | async-done | bytes 1048608 | tf_op jit(solution)/shard_map/all_to_all | solution.py:152
  138.5 0.3 mul.98
  138.9 1.8 multiply_reduce_fusion
  140.9 42.3 %all-gather.1 = bf16[32,1,8192]{2,1,0:T(2,128)(2,1)S(1)} all-gather(bf16[1,1,8192]{2,1,0:T(2,128)(2,1)S(1)} %convert_bitcast_fusion), channel_id=1, replica_groups=mesh['groups'=1,'seq'=32] {'seq'}, dimensions={0}, use_global_device_ids=true | all-gather | bytes 540672 | tf_op jit(solution)/shard_map/all_gather | solution.py:184
  183.3 1.0 fusion.17
  184.2 0.5 broadcast.144
  184.8 0.7 reduce.12
  185.4 8.8 %all_to_all.40 = bf16[32,2,128]{2,1,0:T(2,128)(2,1)S(1)} all-to-all(bf16[32,2,128]{2,1,0:T(2,128)(2,1)S(1)} %reshape.440), channel_id=1, replica_groups=mesh['groups'=1,'seq'=32] {'seq'}, dimensions={0} | all-to-all | bytes 32768 | tf_op jit(solution)/shard_map/all_to_all | solution.py:188
  194.3 0.6 reshape.441
  (81 shorter events, 5.0 us)
Async XLA Ops:
  0.0 113.2 %copy-start = (bf16[1,1024]{1,0:T(2,128)(2,1)S(1)}, bf16[1,1024]{1,0:T(2,128)(2,1)}, u32[]{:S(2)}) copy-start(bf16[1,1024]{1,0:T(2,128)(2,1)} %param.17) | copy-start | bytes 6148
  88.2 24.1 %copy-start.4 = (bf16[1,8192]{1,0:T(2,128)(2,1)S(1)}, bf16[1,8192]{1,0:T(2,128)(2,1)}, u32[]{:S(2)}) copy-start(bf16[1,8192]{1,0:T(2,128)(2,1)} %param.12) | copy-start | bytes 49156
  88.2 24.2 %copy-start.2 = (bf16[1,256,1024]{2,1,0:T(8,128)(2,1)S(1)}, bf16[1,256,1024]{2,1,0:T(8,128)(2,1)}, u32[]{:S(2)}) copy-start(bf16[1,256,1024]{2,1,0:T(8,128)(2,1)} %param.15) | copy-start | bytes 1572868
  88.2 25.8 %copy-start.3 = (bf16[1,256,1024]{2,1,0:T(8,128)(2,1)S(1)}, bf16[1,256,1024]{2,1,0:T(8,128)(2,1)}, u32[]{:S(2)}) copy-start(bf16[1,256,1024]{2,1,0:T(8,128)(2,1)} %param.16) | copy-start | bytes 1572868
  90.3 9.7 %all-to-all-start = ((f32[32,1,64]{2,1,0:T(1,128)}), f32[32,1,64]{2,1,0:T(1,128)S(1)}, u32[]{:S(2)}, u32[]{:S(2)}) async-start(f32[32,1,64]{2,1,0:T(1,128)} %bitcast.26), calls=%async_computation | async-start | bytes 32768 | tf_op jit(solution)/shard_map/all_to_all | solution.py:159
  100.1 9.6 %all-to-all-start.1 = ((f32[32,1,64]{2,1,0:T(1,128)}), f32[32,1,64]{2,1,0:T(1,128)S(1)}, u32[]{:S(2)}, u32[]{:S(2)}) async-start(f32[32,1,64]{2,1,0:T(1,128)} %bitcast.32), calls=%async_computation.1 | async-start | bytes 32768 | tf_op jit(solution)/shard_map/all_to_all | solution.py:162
  102.7 11.5 %copy-start.5 = (bf16[1,1024]{1,0:T(2,128)(2,1)S(1)}, bf16[1,1024]{1,0:T(2,128)(2,1)}, u32[]{:S(2)}) copy-start(bf16[1,1024]{1,0:T(2,128)(2,1)} %param.18) | copy-start | bytes 6148
  109.7 28.9 %all-to-all-start.2 = ((f32[32,1,8192]{2,1,0:T(1,128)}), f32[32,1,8192]{2,1,0:T(1,128)S(1)}, u32[]{:S(2)}, u32[]{:S(2)}) async-start(f32[32,1,8192]{2,1,0:T(1,128)} %reshape.394), calls=%async_computation.2 | async-start | bytes 2097152 | tf_op jit(solution)/shard_map/all_to_all | solution.py:152
  138.5 44.7 %copy-start.1 = (bf16[8192,256]{1,0:T(8,128)(2,1)S(1)}, bf16[8192,256]{1,0:T(8,128)(2,1)}, u32[]{:S(2)}) copy-start(bf16[8192,256]{1,0:T(8,128)(2,1)} %param.21) | copy-start | bytes 12582916
where the time goes:
time: 197 us; the launch traced here: 195 us
  blocking collectives  97.6 us (50%)
  waiting for transfers between devices  33 us (17%)
  local copies, waits for them, and re-layouts  24.8 us (13%)
  matrix products  24.3 us (12%)
  starting transfers between devices  7.75 us (4%)
  other arithmetic  6.5 us (3%)
    all_gather x1, blocking collectives, body(): everyone = lax.all_gather(queries, 'seq', axis=0, tiled=True)  46.4 us
    all_gather x1, blocking collectives, body(): lax.all_gather(attention, 'seq', axis=0, tiled=True)  42.3 us
    all_to_all x1, waiting for transfers between devices, body(): lax.all_to_all(send_part.reshape(all_rows, model_width).astype(jnp.float3...  24 us
    unnamed x20, local copies, waits for them, and re-layouts  14.5 us
    dot_general x8, matrix products, head_scores(): jnp.einsum('rgd,pd->rgp', queries_head, keys_head, preferred_element_type...  11.3 us
    dot_general x8, matrix products, head_scores(): jnp.einsum('rgp,pd->rgd', weights.astype(jnp.bfloat16), values_head, pref...  11.3 us
    all_to_all x1, blocking collectives, body(): lax.all_to_all(panel.astype(jnp.bfloat16), 'seq', split_axis=0, concat_ax...  8.85 us
    all_to_all x1, waiting for transfers between devices, body(): lax.all_to_all(send_max.reshape(all_rows, QUERY_HEADS), 'seq', split_axis...  5.05 us
  transfers between devices with their start and end apart: 3, of which 3 were waited for; matrix products, arithmetic and copies ran while one was open for 3% of the time, Pallas kernels for 0%

commit v1 on v0

v1 whole, which is shorter than its diff:
```python
import functools
import math

import jax
import jax.numpy as jnp
from jax import lax
from jax.experimental import pallas as pl
from jax.experimental.pallas import tpu as pltpu
from jax.sharding import PartitionSpec as P

QUERY_HEADS = 64
KEY_VALUE_HEADS = 8
GROUP = QUERY_HEADS // KEY_VALUE_HEADS
HEAD_SIZE = 128
PROMPT_COUNT = 4
SLOTS = 2
SCALE = 1.0 / math.sqrt(HEAD_SIZE)
SCALE_LOG2 = SCALE * math.log2(math.e)
VMEM = pl.BlockSpec(memory_space=pltpu.VMEM)
SMEM = pl.BlockSpec(memory_space=pltpu.SMEM)
NT = (((1,), (1,)), ((), ()))


def place(segment):
    me = lax.axis_index("seq")
    return me // segment, lax.rem(me, segment)


def each(count, step):
    def one(i, carry):
        step(i + 1)
        return carry

    lax.fori_loop(0, count - 1, one, 0)


def barrier(segment):
    z, j = place(segment)
    sem = pltpu.get_barrier_semaphore()

    def plane(d):
        to = z * segment + lax.rem(j + d, segment)
        pl.semaphore_signal(sem, inc=1, device_id={"seq": to})

    def column(d):
        to = lax.rem(z + d, PROMPT_COUNT) * segment + j
        pl.semaphore_signal(sem, inc=1, device_id={"seq": to})

    each(segment, plane)
    each(PROMPT_COUNT, column)
    pl.semaphore_wait(sem, segment - 1 + PROMPT_COUNT - 1)


def exchange(ref, send, recv, segment, source=None, in_plane=True):
    z, j = place(segment)
    count, mine = (segment, j) if in_plane else (PROMPT_COUNT, z)

    def copy(d, block):
        peer = lax.rem(mine + d, count)
        to = z * segment + peer if in_plane else peer * segment + j
        src = ref.at[mine] if source is None else source.at[peer]
        return pltpu.make_async_remote_copy(
            src_ref=src,
            dst_ref=ref.at[block],
            send_sem=send.at[d],
            recv_sem=recv.at[block],
            device_id={"seq": to},
        )

    def start():
        each(count, lambda d: copy(d, mine).start())

    def wait_recv():
        each(count, lambda d: copy(d, lax.rem(mine + d, count)).wait_recv())

    def wait_send():
        each(count, lambda d: copy(d, mine).wait_send())

    return start, wait_recv, wait_send


def lanes(shape):
    return lax.broadcasted_iota(jnp.int32, shape, len(shape) - 1)


def pick(at, choices):
    at = jnp.full(choices[0].shape, at, jnp.int32)
    out = choices[0]
    for i, choice in enumerate(choices[1:]):
        out = jnp.where(at == i + 1, choice, out)
    return out


def own_suffix(length, q, keys_ref, values_ref, key_ref, value_ref):
    parts = []
    logs = jnp.zeros((GROUP, 128), jnp.float32)
    slots = keys_ref.shape[0]
    live = lanes((GROUP, slots)) < length
    for k in range(KEY_VALUE_HEADS):
        cut = slice(k * HEAD_SIZE, (k + 1) * HEAD_SIZE)
        head = q[k * GROUP : (k + 1) * GROUP]
        scores = lax.dot_general(
            head.astype(jnp.bfloat16), keys_ref[:, cut], NT, preferred_element_type=jnp.float32
        )
        scores = jnp.where(live, scores * SCALE, -1e30)
        fresh = jnp.sum(head * key_ref[:, cut].astype(jnp.float32), axis=1, keepdims=True) * SCALE
        top = jnp.maximum(jnp.max(scores, axis=1, keepdims=True), fresh)
        weights = jnp.exp(scores - top)
        fresh_weight = jnp.exp(fresh - top)
        total = jnp.sum(weights, axis=1, keepdims=True) + fresh_weight
        out = jnp.dot(
            weights.astype(jnp.bfloat16), values_ref[:, cut], preferred_element_type=jnp.float32
        )
        fresh_weight = fresh_weight.astype(jnp.bfloat16).astype(jnp.float32)
        out = out + fresh_weight * value_ref[:, cut].astype(jnp.float32)
        parts.append(out / total)
        logs = jnp.where(lanes(logs.shape) == k, top + jnp.log(total), logs)
    return jnp.concatenate(parts, axis=0), logs


def gather_kernel(
    segment,
    slot_ref,
    length_ref,
    q_ref,
    keys_ref,
    values_ref,
    key_ref,
    value_ref,
    out_ref,
    part_ref,
    logs_ref,
    column,
    sems,
):
    z, j = place(segment)
    barrier(segment)
    column[z] = q_ref[...]
    start, recv, sent = exchange(column, sems.at[0], sems.at[1], segment, in_plane=False)
    start()
    part, logs = own_suffix(
        length_ref[0], q_ref[...].astype(jnp.float32), keys_ref, values_ref, key_ref, value_ref
    )
    part_ref[z] = part.astype(jnp.bfloat16)
    logs_ref[z] = logs
    recv()
    for s in range(SLOTS):
        out_ref[j, s] = pick(slot_ref[s], [column[b] for b in range(PROMPT_COUNT)])
    start2, recv2, sent2 = exchange(out_ref, sems.at[2], sems.at[3], segment)
    start3, recv3, sent3 = exchange(part_ref, sems.at[4], sems.at[5], segment, in_plane=False)
    start4, recv4, sent4 = exchange(logs_ref, sems.at[6], sems.at[7], segment, in_plane=False)
    start2()
    start3()
    start4()
    for wait in (recv2, recv3, recv4, sent, sent2, sent3, sent4):
        wait()


def attend_kernel(q_ref, keys_ref, values_ref, part_ref, logs_ref):
    step = pl.program_id(0)
    segment = q_ref.shape[0]
    rows = segment * SLOTS * GROUP

    @pl.when(step == 0)
    def _():
        logs_ref[...] = jnp.zeros_like(logs_ref)

    q = q_ref[...].astype(jnp.float32).reshape(segment * SLOTS, 2, GROUP, HEAD_SIZE)
    parts = []
    logs = logs_ref[...]
    for h in range(2):
        cut = slice(h * HEAD_SIZE, (h + 1) * HEAD_SIZE)
        head = q[:, h].reshape(rows, HEAD_SIZE).astype(jnp.bfloat16)
        scores = lax.dot_general(head, keys_ref[:, cut], NT, preferred_element_type=jnp.float32)
        top = jnp.max(scores, axis=1, keepdims=True)
        weights = jnp.exp2((scores - top) * SCALE_LOG2)
        total = jnp.sum(weights, axis=1, keepdims=True)
        out = jnp.dot(
            weights.astype(jnp.bfloat16), values_ref[:, cut], preferred_element_type=jnp.float32
        )
        parts.append((out / total).reshape(segment * SLOTS, GROUP, HEAD_SIZE))
        logs = jnp.where(lanes(logs.shape) == step * 2 + h, top * SCALE + jnp.log(total), logs)
    logs_ref[...] = logs
    both = jnp.concatenate(parts, axis=1)
    part_ref[...] = both.astype(jnp.bfloat16).reshape(part_ref.shape)


def spread(weights, pair):
    first = weights[:, 2 * pair : 2 * pair + 1]
    second = weights[:, 2 * pair + 1 : 2 * pair + 2]
    return jnp.concatenate([first, second], axis=0)


def combine_kernel(
    segment,
    index_ref,
    parts_ref,
    logs_ref,
    suffix_ref,
    suffix_logs_ref,
    out_ref,
    got,
    got_logs,
    column,
    column_logs,
    sems,
):
    z, j = place(segment)
    barrier(segment)
    first = exchange(got, sems.at[0], sems.at[1], segment, source=parts_ref)
    first_logs = exchange(got_logs, sems.at[2], sems.at[3], segment, source=logs_ref)
    first[0]()
    first_logs[0]()
    got[j] = parts_ref[j]
    got_logs[j] = logs_ref[j]
    first_logs[1]()
    logs = got_logs[...]
    best = jnp.max(logs, axis=0)
    weights = jnp.exp(logs - best[None])
    total = jnp.sum(weights, axis=0)
    weights = weights / total[None]
    column_logs[z] = best + jnp.log(total)
    first[1]()
    for s in range(SLOTS):
        for pair in range(KEY_VALUE_HEADS // 2):
            rows = slice(pair * 16, pair * 16 + 16)
            acc = jnp.zeros((16, HEAD_SIZE), jnp.float32)
            for i in range(segment):
                w = spread(weights[i, s * GROUP : (s + 1) * GROUP], pair)
                acc = acc + w * got[i, s, rows].astype(jnp.float32)
            column[z, s, rows] = acc.astype(jnp.bfloat16)
    second = exchange(column, sems.at[4], sems.at[5], segment, in_plane=False)
    second_logs = exchange(column_logs, sems.at[6], sems.at[7], segment, in_plane=False)
    second[0]()
    second_logs[0]()
    second_logs[1]()
    second[1]()
    for b in range(PROMPT_COUNT):
        at = index_ref[b]
        prompt = pick(at, [column[i // SLOTS, i % SLOTS] for i in range(PROMPT_COUNT * SLOTS)])
        prompt = prompt.astype(jnp.float32)
        prompt_logs = pick(
            at,
            [
                column_logs[p, s * GROUP : (s + 1) * GROUP]
                for p in range(PROMPT_COUNT)
                for s in range(SLOTS)
            ],
        )
        own_logs = suffix_logs_ref[b]
        best = jnp.maximum(prompt_logs, own_logs)
        prompt_weight = jnp.exp(prompt_logs - best)
        own_weight = jnp.exp(own_logs - best)
        total = prompt_weight + own_weight
        prompt_weight = prompt_weight / total
        own_weight = own_weight / total
        for pair in range(KEY_VALUE_HEADS // 2):
            rows = slice(pair * 16, pair * 16 + 16)
            row = spread(prompt_weight, pair) * prompt[rows]
            row = row + spread(own_weight, pair) * suffix_ref[b, rows].astype(jnp.float32)
            out_ref[j, b, rows] = row.astype(jnp.bfloat16)
    third = exchange(out_ref, sems.at[8], sems.at[9], segment)
    third[0]()
    third[1]()
    for group in (first, first_logs, second, second_logs, third):
        group[2]()


def body(
    queries,
    shared_prompt_keys,
    shared_prompt_values,
    private_cached_keys,
    private_cached_values,
    token_keys,
    token_values,
    suffix_lengths,
    block_prompts,
    out_weight,
):
    n = lax.axis_size("seq")
    segment = n // PROMPT_COUNT
    z, j = place(segment)
    count, width = queries.shape
    assert count == 1 and block_prompts.shape[0] == PROMPT_COUNT
    heads, size = QUERY_HEADS, HEAD_SIZE
    positions = shared_prompt_keys.shape[0]
    bf, f32 = jnp.bfloat16, jnp.float32
    shape = jax.ShapeDtypeStruct

    blocks = jnp.arange(PROMPT_COUNT, dtype=jnp.int32)
    same = block_prompts[:, None] == block_prompts[None, :]
    rank = jnp.sum(same & (blocks[None, :] < blocks[:, None]), axis=1).astype(jnp.int32)
    mine = (block_prompts[None, :] == z) & (rank[None, :] == blocks[:SLOTS, None])
    slot_block = jnp.sum(jnp.where(mine, blocks[None, :], 0), axis=1).astype(jnp.int32)
    index = block_prompts * SLOTS + rank

    most = max(segment, PROMPT_COUNT)
    gathered, suffix, suffix_logs = pl.pallas_call(
        functools.partial(gather_kernel, segment),
        out_shape=(
            shape((segment, SLOTS, heads, size), bf),
            shape((PROMPT_COUNT, heads, size), bf),
            shape((PROMPT_COUNT, GROUP, 128), f32),
        ),
        in_specs=[SMEM, SMEM] + [VMEM] * 5,
        out_specs=(VMEM, VMEM, VMEM),
        scratch_shapes=[
            pltpu.VMEM((PROMPT_COUNT, heads, size), bf),
            pltpu.SemaphoreType.DMA((8, most)),
        ],
        compiler_params=pltpu.CompilerParams(
            collective_id=0, has_side_effects=True, vmem_limit_bytes=24 << 20
        ),
    )(
        slot_block,
        suffix_lengths,
        queries.reshape(heads, size),
        private_cached_keys[0],
        private_cached_values[0],
        token_keys,
        token_values,
    )

    rows = segment * SLOTS * GROUP
    parts, logs = pl.pallas_call(
        attend_kernel,
        out_shape=(shape((segment, SLOTS, heads, size), bf), shape((rows, 128), f32)),
        grid=(KEY_VALUE_HEADS // 2,),
        in_specs=[
            pl.BlockSpec((segment, SLOTS, 16, size), lambda i: (0, 0, i, 0)),
            pl.BlockSpec((positions, 2 * size), lambda i: (0, i)),
            pl.BlockSpec((positions, 2 * size), lambda i: (0, i)),
        ],
        out_specs=(
            pl.BlockSpec((segment, SLOTS, 16, size), lambda i: (0, 0, i, 0)),
            pl.BlockSpec((rows, 128), lambda i: (0, 0)),
        ),
        compiler_params=pltpu.CompilerParams(vmem_limit_bytes=44 << 20),
    )(gathered, shared_prompt_keys, shared_prompt_values)

    attention = pl.pallas_call(
        functools.partial(combine_kernel, segment),
        out_shape=shape((segment, PROMPT_COUNT, heads, size), bf),
        in_specs=[SMEM] + [VMEM] * 4,
        out_specs=VMEM,
        scratch_shapes=[
            pltpu.VMEM((segment, SLOTS, heads, size), bf),
            pltpu.VMEM((segment, SLOTS * GROUP, 128), f32),
            pltpu.VMEM((PROMPT_COUNT, SLOTS, heads, size), bf),
            pltpu.VMEM((PROMPT_COUNT, SLOTS * GROUP, 128), f32),
            pltpu.SemaphoreType.DMA((10, most)),
        ],
        compiler_params=pltpu.CompilerParams(
            collective_id=1, has_side_effects=True, vmem_limit_bytes=24 << 20
        ),
    )(index, parts, logs.reshape(segment, SLOTS * GROUP, 128), suffix, suffix_logs)

    panel = jnp.dot(
        attention.reshape(n, width), out_weight, preferred_element_type=f32
    ).astype(bf)
    panel = panel.reshape(segment, PROMPT_COUNT, -1).transpose(1, 0, 2).reshape(n, -1)
    return lax.all_to_all(panel, "seq", split_axis=0, concat_axis=1, tiled=True)


def solution(mesh):
    in_specs = (
        P(("groups", "seq"), None),
        P(("groups", "seq"), None),
        P(("groups", "seq"), None),
        P(("groups", "seq"), None, None),
        P(("groups", "seq"), None, None),
        P(("groups", "seq"), None),
        P(("groups", "seq"), None),
        P(("groups", "seq")),
        P("groups"),
        P(None, "seq"),
    )
    out_specs = P(("groups", "seq"), None)
    return jax.shard_map(body, mesh=mesh, in_specs=in_specs, out_specs=out_specs, check_vma=False)
```

time: 197 us -> 68.2 us (0.35)
  blocking collectives: 97.6 us -> 11.1 us
  Pallas kernels: 0 us -> 42.1 us
  waiting for transfers between devices: 33 us -> 0 us
  matrix products: 24.3 us -> 0.81 us
  local copies, waits for them, and re-layouts: 24.8 us -> 9 us
  starting transfers between devices: 7.75 us -> 0 us
  other arithmetic: 6.5 us -> 3.92 us
    all_gather x2 -> x0, blocking collectives: 88.8 us -> none  [the longest x1 46.4 us: body(): everyone = lax.all_gather(queries, 'seq', axis=0, tiled=True)]
    pallas_call x0 -> x3, Pallas kernels: none -> 42.1 us  [the longest x1 21.6 us: body(): pl.pallas_call(functools.partial(combine_kernel, segment), out_shape=shap...]
    all_to_all x3 -> x0, waiting for transfers between devices: 33 us -> none  [the longest x1 24 us: body(): lax.all_to_all(send_part.reshape(all_rows, model_width).astype(jnp.float3...]
    dot_general x20 -> x1, matrix products: 24.3 us -> 0.81 us  [body(): jnp.dot(attention.reshape(n, width), out_weight, preferred_element_type=f32)]
    all_to_all x3 -> x0, starting transfers between devices: 7.75 us -> none  [the longest x1 2.64 us: body(): lax.all_to_all(send_part.reshape(all_rows, model_width).astype(jnp.float3...]
    unnamed x20 -> x16, local copies, waits for them, and re-layouts: 14.5 us -> 8.46 us
    reduce_sum x12 -> x2, other arithmetic: 4.5 us -> 1.1 us  [the longest x1 0.91 us: body(): jnp.sum(same & (blocks[None, :] < blocks[:, None]), axis=1)]
    scatter x3 -> x0, local copies, waits for them, and re-layouts: 3.24 us -> none  [the longest x1 1.31 us: body(): send_total = jnp.zeros((blocks, rows_in_block, QUERY_HEADS), jnp.float32)...]
  transfers between devices with their start and end apart: 3 -> 0, of which waited for: 3 -> 0; matrix products, arithmetic and copies ran while one was open for 3% -> 0% of each run, Pallas kernels for 0% -> 0%
where the time goes in v1:
time: 68.2 us; the launch traced here: 67.7 us
  Pallas kernels  42.1 us (62%)
  blocking collectives  11.1 us (16%)
  local copies, waits for them, and re-layouts  9 us (13%)
  other arithmetic  3.92 us (6%)
  matrix products  0.81 us (1%)
  between operations  0.75 us (1%)
    pallas_call x1, Pallas kernels, body(): pl.pallas_call(functools.partial(combine_kernel, segment), out_shape=shap...  21.6 us
    pallas_call x1, Pallas kernels, body(): pl.pallas_call(functools.partial(gather_kernel, segment), out_shape=(shap...  14.4 us
    all_to_all x1, blocking collectives, body(): return lax.all_to_all(panel, 'seq', split_axis=0, concat_axis=1, tiled=True)  11.1 us
    unnamed x16, local copies, waits for them, and re-layouts  8.46 us
    pallas_call x1, Pallas kernels, body(): pl.pallas_call(attend_kernel, out_shape=(shape((segment, SLOTS, heads, si...  6.09 us

profile of v1, /device:TPU:0, one launch (start us, length us, event | category | flops | bytes accessed | tf_op | source)
XLA Modules:
  0.0 67.7 jit_solution(8730997971602093254)
XLA Ops:
  0.0 0.9 %convert_reduce_fusion = s32[4]{0:T(128)S(1)} fusion(s32[4]{0:T(128)} %param.18), kind=kLoop, calls=%fused_computation.4 | loop fusion | flops 76 | bytes 32 | tf_op jit(solution)/shard_map/reduce_sum | solution.py:293
  0.9 0.7 broadcast_compare_fusion
  2.2 0.7 multiply_add_fusion.index_ref
  2.9 0.2 fusion.3.slot_ref
  3.1 0.8 %reduce = bf16[8192]{0:T(1024)(128)(2,1)S(1)} reduce(bf16[1,8192]{1,0:T(2,128)(2,1)} %param.10, bf16[]{:T(256)} %constant.29), dimensions={0}, to_apply=%param.10.reduce_sub_computation | reduce | bytes 32770 | tf_op args[0]
  3.9 0.0 copy-start.2
  4.0 1.0 %copy-done.2 = bf16[1,256,1024]{2,1,0:T(8,128)(2,1)S(1)} copy-done((bf16[1,256,1024]{2,1,0:T(8,128)(2,1)S(1)}, bf16[1,256,1024]{2,1,0:T(8,128)(2,1)}, u32[]{:S(2)}) %copy-start.2) | copy-done | bytes 524312
  5.0 0.0 copy-start.3
  5.0 1.0 %copy-done.3 = bf16[1,256,1024]{2,1,0:T(8,128)(2,1)S(1)} copy-done((bf16[1,256,1024]{2,1,0:T(8,128)(2,1)S(1)}, bf16[1,256,1024]{2,1,0:T(8,128)(2,1)}, u32[]{:S(2)}) %copy-start.3) | copy-done | bytes 524312
  6.0 0.0 copy-start.4
  6.0 0.7 %copy-done.4 = bf16[1,1024]{1,0:T(2,128)(2,1)S(1)} copy-done((bf16[1,1024]{1,0:T(2,128)(2,1)S(1)}, bf16[1,1024]{1,0:T(2,128)(2,1)}, u32[]{:S(2)}) %copy-start.4) | copy-done | bytes 2072
  6.7 0.0 copy-start.5
  6.7 0.7 %copy-done.5 = bf16[1,1024]{1,0:T(2,128)(2,1)S(1)} copy-done((bf16[1,1024]{1,0:T(2,128)(2,1)S(1)}, bf16[1,1024]{1,0:T(2,128)(2,1)}, u32[]{:S(2)}) %copy-start.5) | copy-done | bytes 2072
  7.4 14.4 %shard_map.100 = (bf16[8,2,64,128]{3,2,1,0:T(8,128)(2,1)S(1)}, bf16[4,64,128]{2,1,0:T(8,128)(2,1)S(1)}, f32[4,8,128]{2,1,0:T(8,128)S(1)}) custom-call(s32[2]{0:T(128)S(1)} %fusion.3.slot_ref, s32[1]{0:T(128)S(6)} %copy.24.length_ref, bf16[64,128]{1,0:T(8,128)(2,1)S(1)} %bitcast.20, bf16[256,1024]{1,0:T(8,128)(2,1)S(1)} %bitcast.18, ...), custom_call_target="tpu_custom_call" | custom-call | tf_op jit(solution)/shard_map/pallas_call | solution.py:299
  21.8 0.0 copy-start
  21.8 2.2 %copy-done = bf16[2048,1024]{1,0:T(8,128)(2,1)S(1)} copy-done((bf16[2048,1024]{1,0:T(8,128)(2,1)S(1)}, bf16[2048,1024]{1,0:T(8,128)(2,1)}, u32[]{:S(2)}) %copy-start) | copy-done | bytes 4194328
  24.0 0.0 copy-start.1
  24.0 2.2 %copy-done.1 = bf16[2048,1024]{1,0:T(8,128)(2,1)S(1)} copy-done((bf16[2048,1024]{1,0:T(8,128)(2,1)S(1)}, bf16[2048,1024]{1,0:T(8,128)(2,1)}, u32[]{:S(2)}) %copy-start.1) | copy-done | bytes 4194328
  26.2 0.0 copy-start.6
  26.2 6.1 %shard_map.101 = (bf16[8,2,64,128]{3,2,1,0:T(8,128)(2,1)S(1)}, f32[128,128]{1,0:T(8,128)S(1)}) custom-call(bf16[8,2,64,128]{3,2,1,0:T(8,128)(2,1)S(1)} %get-tuple-element.10.q_ref, bf16[2048,1024]{1,0:T(8,128)(2,1)S(1)} %copy-done, bf16[2048,1024]{1,0:T(8,128)(2,1)S(1)} %copy-done.1), custom_call_target="tpu_custom_call" | custom-call | tf_op jit(solution)/shard_map/pallas_call | solution.py:326
  32.3 21.6 %shard_map.102 = bf16[8,4,64,128]{3,2,1,0:T(8,128)(2,1)S(1)} custom-call(s32[4]{0:T(128)S(1)} %multiply_add_fusion.index_ref, bf16[8,2,64,128]{3,2,1,0:T(8,128)(2,1)S(1)} %get-tuple-element.11.parts_ref, f32[8,16,128]{2,1,0:T(8,128)S(1)} %bitcast.21, bf16[4,64,128]{2,1,0:T(8,128)(2,1)S(1)} %get-tuple-element.13.suffix_ref, ...), custom_call_target="tpu_custom_call" | custom-call | tf_op jit(solution)/shard_map/pallas_call | solution.py:342
  53.9 0.0 copy-done.6
  53.9 0.8 %convolution_convert_fusion = bf16[32,256]{1,0:T(8,128)(2,1)S(1)} fusion(bf16[8192,256]{1,0:T(8,128)(2,1)S(1)} %copy-done.6, bf16[4,8,64,128]{3,2,1,0:T(8,128)(2,1)S(1)} %bitcast.17), kind=kOutput, calls=%fused_computation | convolution fusion | flops 134225920 | bytes 4734976 | tf_op jit(solution)/shard_map/dot_general | solution.py:359
  54.7 0.5 broadcast.13
  55.3 0.7 reduce.1
  55.9 11.1 %all_to_all.16 = bf16[32,2,128]{2,1,0:T(2,128)(2,1)S(1)} all-to-all(bf16[32,2,128]{2,1,0:T(2,128)(2,1)S(1)} %reshape.31), channel_id=1, replica_groups=mesh['groups'=1,'seq'=32] {'seq'}, dimensions={0} | all-to-all | bytes 32768 | tf_op jit(solution)/shard_map/all_to_all | solution.py:363
  67.1 0.6 reshape.32
  (4 shorter events, 0.0 us)
Async XLA Ops:
  3.9 1.0 %copy-start.2 = (bf16[1,256,1024]{2,1,0:T(8,128)(2,1)S(1)}, bf16[1,256,1024]{2,1,0:T(8,128)(2,1)}, u32[]{:S(2)}) copy-start(bf16[1,256,1024]{2,1,0:T(8,128)(2,1)} %param.13) | copy-start | bytes 1572868
  5.0 1.0 %copy-start.3 = (bf16[1,256,1024]{2,1,0:T(8,128)(2,1)S(1)}, bf16[1,256,1024]{2,1,0:T(8,128)(2,1)}, u32[]{:S(2)}) copy-start(bf16[1,256,1024]{2,1,0:T(8,128)(2,1)} %param.14) | copy-start | bytes 1572868
  6.0 0.7 %copy-start.4 = (bf16[1,1024]{1,0:T(2,128)(2,1)S(1)}, bf16[1,1024]{1,0:T(2,128)(2,1)}, u32[]{:S(2)}) copy-start(bf16[1,1024]{1,0:T(2,128)(2,1)} %key_ref.1) | copy-start | bytes 6148
  6.7 0.7 %copy-start.5 = (bf16[1,1024]{1,0:T(2,128)(2,1)S(1)}, bf16[1,1024]{1,0:T(2,128)(2,1)}, u32[]{:S(2)}) copy-start(bf16[1,1024]{1,0:T(2,128)(2,1)} %value_ref.1) | copy-start | bytes 6148
  21.8 2.2 %copy-start = (bf16[2048,1024]{1,0:T(8,128)(2,1)S(1)}, bf16[2048,1024]{1,0:T(8,128)(2,1)}, u32[]{:S(2)}) copy-start(bf16[2048,1024]{1,0:T(8,128)(2,1)} %keys_ref.1) | copy-start | bytes 12582916
  24.0 2.2 %copy-start.1 = (bf16[2048,1024]{1,0:T(8,128)(2,1)S(1)}, bf16[2048,1024]{1,0:T(8,128)(2,1)}, u32[]{:S(2)}) copy-start(bf16[2048,1024]{1,0:T(8,128)(2,1)} %values_ref.1) | copy-start | bytes 12582916
  26.2 27.7 %copy-start.6 = (bf16[8192,256]{1,0:T(8,128)(2,1)S(1)}, bf16[8192,256]{1,0:T(8,128)(2,1)}, u32[]{:S(2)}) copy-start(bf16[8192,256]{1,0:T(8,128)(2,1)} %param.19) | copy-start | bytes 12582916

commit v2 on v1

v2 whole, which is shorter than its diff:
```python
import functools
import math

import jax
import jax.numpy as jnp
from jax import lax
from jax.experimental import pallas as pl
from jax.experimental.pallas import tpu as pltpu
from jax.sharding import PartitionSpec as P

QUERY_HEADS = 64
KEY_VALUE_HEADS = 8
GROUP = QUERY_HEADS // KEY_VALUE_HEADS
HEAD_SIZE = 128
PROMPT_COUNT = 4
SLOTS = 2
SCALE = 1.0 / math.sqrt(HEAD_SIZE)
SCALE_LOG2 = SCALE * math.log2(math.e)
VMEM = pl.BlockSpec(memory_space=pltpu.VMEM)
ANY = pl.BlockSpec(memory_space=pl.ANY)
SMEM = pl.BlockSpec(memory_space=pltpu.SMEM)
NT = (((1,), (1,)), ((), ()))


def place(segment):
    me = lax.axis_index("seq")
    return me // segment, lax.rem(me, segment)


def each(count, step):
    def one(i, carry):
        step(i + 1)
        return carry

    lax.fori_loop(0, count - 1, one, 0)


def greet(segment):
    z, j = place(segment)
    sem = pltpu.get_barrier_semaphore()

    def plane(d):
        to = z * segment + lax.rem(j + d, segment)
        pl.semaphore_signal(sem, inc=1, device_id={"seq": to})

    def column(d):
        to = lax.rem(z + d, PROMPT_COUNT) * segment + j
        pl.semaphore_signal(sem, inc=1, device_id={"seq": to})

    each(segment, plane)
    each(PROMPT_COUNT, column)


def greeted(segment):
    pl.semaphore_wait(pltpu.get_barrier_semaphore(), segment - 1 + PROMPT_COUNT - 1)


def exchange(ref, send, recv, segment, source=None, in_plane=True, rows=None):
    z, j = place(segment)
    count, mine = (segment, j) if in_plane else (PROMPT_COUNT, z)

    def view(array, block):
        return array.at[block] if rows is None else array.at[block, :, rows]

    def copy(d, block):
        peer = lax.rem(mine + d, count)
        to = z * segment + peer if in_plane else peer * segment + j
        return pltpu.make_async_remote_copy(
            src_ref=view(ref, mine) if source is None else view(source, peer),
            dst_ref=view(ref, block),
            send_sem=send.at[d],
            recv_sem=recv.at[block],
            device_id={"seq": to},
        )

    def start():
        each(count, lambda d: copy(d, mine).start())

    def wait_recv():
        each(count, lambda d: copy(d, lax.rem(mine + d, count)).wait_recv())

    def wait_send():
        each(count, lambda d: copy(d, mine).wait_send())

    return start, wait_recv, wait_send


def lanes(shape):
    return lax.broadcasted_iota(jnp.int32, shape, len(shape) - 1)


def pick(at, choices):
    at = jnp.full(choices[0].shape, at, jnp.int32)
    out = choices[0]
    for i, choice in enumerate(choices[1:]):
        out = jnp.where(at == i + 1, choice, out)
    return out


def own_suffix(length, q, keys_ref, values_ref, key_ref, value_ref):
    parts = []
    logs = jnp.zeros((GROUP, 128), jnp.float32)
    slots = keys_ref.shape[0]
    live = lanes((GROUP, slots)) < length
    for k in range(KEY_VALUE_HEADS):
        cut = slice(k * HEAD_SIZE, (k + 1) * HEAD_SIZE)
        head = q[k * GROUP : (k + 1) * GROUP]
        scores = lax.dot_general(
            head.astype(jnp.bfloat16), keys_ref[:, cut], NT, preferred_element_type=jnp.float32
        )
        scores = jnp.where(live, scores * SCALE, -1e30)
        fresh = jnp.sum(head * key_ref[:, cut].astype(jnp.float32), axis=1, keepdims=True) * SCALE
        top = jnp.maximum(jnp.max(scores, axis=1, keepdims=True), fresh)
        weights = jnp.exp(scores - top)
        fresh_weight = jnp.exp(fresh - top)
        total = jnp.sum(weights, axis=1, keepdims=True) + fresh_weight
        out = jnp.dot(
            weights.astype(jnp.bfloat16), values_ref[:, cut], preferred_element_type=jnp.float32
        )
        fresh_weight = fresh_weight.astype(jnp.bfloat16).astype(jnp.float32)
        out = out + fresh_weight * value_ref[:, cut].astype(jnp.float32)
        parts.append(out / total)
        logs = jnp.where(lanes(logs.shape) == k, top + jnp.log(total), logs)
    return jnp.concatenate(parts, axis=0), logs


def spread(weights, pair):
    first = weights[:, 2 * pair : 2 * pair + 1]
    second = weights[:, 2 * pair + 1 : 2 * pair + 2]
    return jnp.concatenate([first, second], axis=0)


def pair_rows(i):
    return pl.ds(pl.multiple_of(i * 16, 16), 16)


def attend(i, segment, q_ref, keys_ref, values_ref, part_ref, logs_ref):
    rows = segment * SLOTS * GROUP
    q = q_ref[:, :, pair_rows(i), :].astype(jnp.float32)
    q = q.reshape(segment * SLOTS, 2, GROUP, HEAD_SIZE)
    parts = []
    logs = logs_ref[...].reshape(rows, 128)
    for h in range(2):
        cut = pl.ds(pl.multiple_of((i * 2 + h) * HEAD_SIZE, HEAD_SIZE), HEAD_SIZE)
        head = q[:, h].reshape(rows, HEAD_SIZE).astype(jnp.bfloat16)
        scores = lax.dot_general(head, keys_ref[:, cut], NT, preferred_element_type=jnp.float32)
        top = jnp.max(scores, axis=1, keepdims=True)
        weights = jnp.exp2((scores - top) * SCALE_LOG2)
        total = jnp.sum(weights, axis=1, keepdims=True)
        out = jnp.dot(
            weights.astype(jnp.bfloat16), values_ref[:, cut], preferred_element_type=jnp.float32
        )
        parts.append((out / total).reshape(segment * SLOTS, GROUP, HEAD_SIZE))
        logs = jnp.where(lanes(logs.shape) == i * 2 + h, top * SCALE + jnp.log(total), logs)
    logs_ref[...] = logs.reshape(logs_ref.shape)
    both = jnp.concatenate(parts, axis=1).astype(jnp.bfloat16)
    part_ref[:, :, pair_rows(i), :] = both.reshape(segment, SLOTS, 16, HEAD_SIZE)


def kernel(
    segment,
    prompts_ref,
    length_ref,
    q_ref,
    key_ref,
    value_ref,
    own_keys_hbm,
    own_values_hbm,
    keys_hbm,
    values_hbm,
    weight_hbm,
    out_ref,
    own_keys,
    own_values,
    keys,
    values,
    weight,
    q_column,
    q_all,
    suffix,
    suffix_logs,
    parts,
    logs,
    got,
    got_logs,
    column,
    column_logs,
    rows_all,
    rows_wide,
    panel,
    panel_column,
    panel_rows,
    local_sems,
    sems,
    chunk_sems,
):
    z, j = place(segment)
    n = segment * PROMPT_COUNT
    greet(segment)
    loads = [
        pltpu.make_async_copy(src, dst, local_sems.at[i])
        for i, (src, dst) in enumerate(
            (
                (own_keys_hbm, own_keys),
                (own_values_hbm, own_values),
                (keys_hbm, keys),
                (values_hbm, values),
                (weight_hbm, weight),
            )
        )
    ]
    for load in loads:
        load.start()

    flat = q_ref[...].astype(jnp.float32)
    q = jnp.concatenate(
        [flat[:, h * HEAD_SIZE : (h + 1) * HEAD_SIZE] for h in range(QUERY_HEADS)], axis=0
    )
    q_column[z] = q.astype(jnp.bfloat16)
    logs[...] = jnp.zeros_like(logs)
    prompts = [prompts_ref[b] for b in range(PROMPT_COUNT)]
    ranks = []
    for b in range(PROMPT_COUNT):
        rank = jnp.int32(0)
        for c in range(b):
            rank = rank + jnp.where(prompts[c] == prompts[b], 1, 0)
        ranks.append(rank)
    slot_block = []
    for s in range(SLOTS):
        block = jnp.int32(0)
        for b in range(PROMPT_COUNT):
            block = jnp.where((prompts[b] == z) & (ranks[b] == s), b, block)
        slot_block.append(block)

    greeted(segment)
    ask = exchange(q_column, sems.at[0], sems.at[1], segment, in_plane=False)
    ask[0]()
    loads[0].wait()
    loads[1].wait()
    part, own_logs = own_suffix(length_ref[0], q, own_keys, own_values, key_ref, value_ref)
    suffix[z] = part
    suffix_logs[z] = own_logs
    ask[1]()
    for s in range(SLOTS):
        q_all[j, s] = pick(slot_block[s], [q_column[b] for b in range(PROMPT_COUNT)])

    def ask_plane(i):
        return exchange(
            q_all, chunk_sems.at[0, i], chunk_sems.at[1, i], segment, rows=pair_rows(i)
        )

    def answer(i):
        return exchange(
            got,
            chunk_sems.at[2, i],
            chunk_sems.at[3, i],
            segment,
            source=parts,
            rows=pair_rows(i),
        )

    pairs = KEY_VALUE_HEADS // 2

    def all_pairs(step):
        def one(i, carry):
            step(i)
            return carry

        lax.fori_loop(0, pairs, one, 0)

    all_pairs(lambda i: ask_plane(i)[0]())
    tell = exchange(suffix, sems.at[2], sems.at[3], segment, in_plane=False)
    tell_logs = exchange(suffix_logs, sems.at[4], sems.at[5], segment, in_plane=False)
    tell[0]()
    tell_logs[0]()
    loads[2].wait()
    loads[3].wait()

    def work(i):
        ask_plane(i)[1]()
        attend(i, segment, q_all, keys, values, parts, logs)
        answer(i)[0]()

    all_pairs(work)
    answer_logs = exchange(got_logs, sems.at[6], sems.at[7], segment, source=logs)
    answer_logs[0]()
    got[j] = parts[j]
    got_logs[j] = logs[j]
    answer_logs[1]()
    all_logs = got_logs[...]
    best = jnp.max(all_logs, axis=0)
    weights = jnp.exp(all_logs - best[None])
    total = jnp.sum(weights, axis=0)
    weights = weights / total[None]
    column_logs[z] = best + jnp.log(total)
    all_pairs(lambda i: answer(i)[1]())
    for s in range(SLOTS):
        for pair in range(pairs):
            rows = slice(pair * 16, pair * 16 + 16)
            acc = jnp.zeros((16, HEAD_SIZE), jnp.float32)
            for i in range(segment):
                w = spread(weights[i, s * GROUP : (s + 1) * GROUP], pair)
                acc = acc + w * got[i, s, rows].astype(jnp.float32)
            column[z, s, rows] = acc.astype(jnp.bfloat16)
    share = exchange(column, sems.at[8], sems.at[9], segment, in_plane=False)
    share_logs = exchange(column_logs, sems.at[10], sems.at[11], segment, in_plane=False)
    share_logs[0]()
    share[0]()
    tell_logs[1]()
    tell[1]()
    share_logs[1]()
    share[1]()
    for b in range(PROMPT_COUNT):
        at = prompts[b] * SLOTS + ranks[b]
        prompt = pick(at, [column[i // SLOTS, i % SLOTS] for i in range(PROMPT_COUNT * SLOTS)])
        prompt = prompt.astype(jnp.float32)
        prompt_logs = pick(
            at,
            [
                column_logs[p, s * GROUP : (s + 1) * GROUP]
                for p in range(PROMPT_COUNT)
                for s in range(SLOTS)
            ],
        )
        own_logs = suffix_logs[b]
        best = jnp.maximum(prompt_logs, own_logs)
        prompt_weight = jnp.exp(prompt_logs - best)
        own_weight = jnp.exp(own_logs - best)
        total = prompt_weight + own_weight
        prompt_weight = prompt_weight / total
        own_weight = own_weight / total
        for pair in range(pairs):
            rows = slice(pair * 16, pair * 16 + 16)
            row = spread(prompt_weight, pair) * prompt[rows]
            row = row + spread(own_weight, pair) * suffix[b, rows]
            rows_all[j, b, rows] = row.astype(jnp.bfloat16)
    gather = exchange(rows_all, sems.at[12], sems.at[13], segment)
    gather[0]()
    loads[4].wait()
    gather[1]()

    def widen(i, carry):
        for b in range(PROMPT_COUNT):
            at = pl.multiple_of((b * segment + i) * QUERY_HEADS, QUERY_HEADS)
            rows_wide[pl.ds(at, QUERY_HEADS), :] = rows_all[i, b].astype(jnp.float32)
        return carry

    lax.fori_loop(0, segment, widen, 0)

    def project(i, acc):
        for pair in range(4):
            h = i * 8 + pair * 2
            both = [rows_wide[pl.ds(h + o, n, stride=QUERY_HEADS), :] for o in range(2)]
            left = jnp.concatenate(both, axis=1).astype(jnp.bfloat16)
            at = pl.multiple_of(h * HEAD_SIZE, 2 * HEAD_SIZE)
            right = weight[pl.ds(at, 2 * HEAD_SIZE), :]
            acc = acc + jnp.dot(left, right, preferred_element_type=jnp.float32)
        return acc

    acc = lax.fori_loop(
        0, QUERY_HEADS // 8, project, jnp.zeros((n, weight.shape[1]), jnp.float32)
    )
    panel[...] = acc.reshape(panel.shape)
    back = exchange(panel_column, sems.at[14], sems.at[15], segment, source=panel, in_plane=False)
    back[0]()
    panel_column[z] = panel[z]
    back[1]()
    for i in range(segment):
        for p in range(PROMPT_COUNT):
            panel_rows[i, p : p + 1, :] = panel_column[p, i : i + 1, :]
    home = exchange(out_ref, sems.at[16], sems.at[17], segment, source=panel_rows)
    home[0]()
    out_ref[j] = panel_rows[j]
    home[1]()
    for group in (ask, tell, tell_logs, answer_logs, share, share_logs, gather, back, home):
        group[2]()
    all_pairs(lambda i: ask_plane(i)[2]())
    all_pairs(lambda i: answer(i)[2]())


def body(
    queries,
    shared_prompt_keys,
    shared_prompt_values,
    private_cached_keys,
    private_cached_values,
    token_keys,
    token_values,
    suffix_lengths,
    block_prompts,
    out_weight,
):
    n = lax.axis_size("seq")
    segment = n // PROMPT_COUNT
    count, width = queries.shape
    assert count == 1 and block_prompts.shape[0] == PROMPT_COUNT
    heads, size = QUERY_HEADS, HEAD_SIZE
    columns = out_weight.shape[1]
    bf, f32 = jnp.bfloat16, jnp.float32
    most = max(segment, PROMPT_COUNT)
    own_keys, own_values = private_cached_keys[0], private_cached_values[0]
    out = pl.pallas_call(
        functools.partial(kernel, segment),
        out_shape=jax.ShapeDtypeStruct((segment, PROMPT_COUNT, columns), f32),
        in_specs=[SMEM, SMEM] + [VMEM] * 3 + [ANY] * 5,
        out_specs=VMEM,
        scratch_shapes=[
            pltpu.VMEM(own_keys.shape, bf),
            pltpu.VMEM(own_values.shape, bf),
            pltpu.VMEM(shared_prompt_keys.shape, bf),
            pltpu.VMEM(shared_prompt_values.shape, bf),
            pltpu.VMEM(out_weight.shape, bf),
            pltpu.VMEM((PROMPT_COUNT, heads, size), bf),
            pltpu.VMEM((segment, SLOTS, heads, size), bf),
            pltpu.VMEM((PROMPT_COUNT, heads, size), f32),
            pltpu.VMEM((PROMPT_COUNT, GROUP, 128), f32),
            pltpu.VMEM((segment, SLOTS, heads, size), bf),
            pltpu.VMEM((segment, SLOTS * GROUP, 128), f32),
            pltpu.VMEM((segment, SLOTS, heads, size), bf),
            pltpu.VMEM((segment, SLOTS * GROUP, 128), f32),
            pltpu.VMEM((PROMPT_COUNT, SLOTS, heads, size), bf),
            pltpu.VMEM((PROMPT_COUNT, SLOTS * GROUP, 128), f32),
            pltpu.VMEM((segment, PROMPT_COUNT, heads, size), bf),
            pltpu.VMEM((n * heads, size), f32),
            pltpu.VMEM((PROMPT_COUNT, segment, columns), f32),
            pltpu.VMEM((PROMPT_COUNT, segment, columns), f32),
            pltpu.VMEM((segment, PROMPT_COUNT, columns), f32),
            pltpu.SemaphoreType.DMA((5,)),
            pltpu.SemaphoreType.DMA((18, most)),
            pltpu.SemaphoreType.DMA((4, KEY_VALUE_HEADS // 2, most)),
        ],
        compiler_params=pltpu.CompilerParams(
            collective_id=0, has_side_effects=True, vmem_limit_bytes=56 << 20
        ),
    )(
        block_prompts,
        suffix_lengths,
        queries,
        token_keys,
        token_values,
        own_keys,
        own_values,
        shared_prompt_keys,
        shared_prompt_values,
        out_weight,
    )
    return out.transpose(1, 0, 2).reshape(1, width).astype(bf)


def solution(mesh):
    in_specs = (
        P(("groups", "seq"), None),
        P(("groups", "seq"), None),
        P(("groups", "seq"), None),
        P(("groups", "seq"), None, None),
        P(("groups", "seq"), None, None),
        P(("groups", "seq"), None),
        P(("groups", "seq"), None),
        P(("groups", "seq")),
        P("groups"),
        P(None, "seq"),
    )
    out_specs = P(("groups", "seq"), None)
    return jax.shard_map(body, mesh=mesh, in_specs=in_specs, out_specs=out_specs, check_vma=False)
```

time: 68.2 us -> 50.5 us (0.74)
  blocking collectives: 11.1 us -> 0 us
  local copies, waits for them, and re-layouts: 9 us -> 0.64 us
  Pallas kernels: 42.1 us -> 48.2 us
  other arithmetic: 3.92 us -> 0.77 us
  matrix products: 0.81 us -> 0 us
    all_to_all x1 -> x0, blocking collectives: 11.1 us -> none  [body(): return lax.all_to_all(panel, 'seq', split_axis=0, concat_axis=1, tiled=True)]
    unnamed x16 -> x0, local copies, waits for them, and re-layouts: 8.46 us -> none
    pallas_call x3 -> x1, Pallas kernels: 42.1 us -> 48.2 us  [body(): pl.pallas_call(functools.partial(kernel, segment), out_shape=jax.ShapeDty...]
    reduce_sum x2 -> x0, other arithmetic: 1.1 us -> none  [the longest x1 0.91 us: body(): jnp.sum(same & (blocks[None, :] < blocks[:, None]), axis=1)]
    unnamed x1 -> x0, other arithmetic: 0.85 us -> none
    dot_general x1 -> x0, matrix products: 0.81 us -> none  [body(): jnp.dot(attention.reshape(n, width), out_weight, preferred_element_type=f32)]
    convert_element_type x0 -> x1, other arithmetic: none -> 0.77 us  [body(): return out.transpose(1, 0, 2).reshape(1, width).astype(bf)]
where the time goes in v2:
time: 50.5 us; the launch traced here: 50.3 us
  Pallas kernels  48.2 us (95%)
  other arithmetic  0.77 us (2%)
  between operations  0.66 us (1%)
  local copies, waits for them, and re-layouts  0.64 us (1%)
    pallas_call x1, Pallas kernels, body(): pl.pallas_call(functools.partial(kernel, segment), out_shape=jax.ShapeDty...  48.2 us

profile of v2, /device:TPU:0, one launch (start us, length us, event | category | flops | bytes accessed | tf_op | source)
XLA Modules:
  0.0 50.3 jit_solution(7702627350938183048)
XLA Ops:
  0.7 48.2 %shard_map.100 = f32[8,4,256]{2,1,0:T(4,128)} custom-call(s32[4]{0:T(128)} %prompts_ref.1, s32[1]{0:T(128)S(6)} %copy.12.length_ref, bf16[1,8192]{1,0:T(2,128)(2,1)} %q_ref.1, bf16[1,1024]{1,0:T(2,128)(2,1)} %key_ref.1, bf16[1,1024]{1,0:T(2,128)(2,1)} %value_ref.1, bf16[256,1024]{1,0:T(8,128)(2,1)} %bitcast.4, bf16[256,1024]{1,0:T(8,128)(2,1)} %bitcast.5, ...), custom_call_target="tpu_custom_call" | custom-call | tf_op jit(solution)/shard_map/pallas_call | solution.py:402
  48.9 0.8 %convert_bitcast_fusion = bf16[4,8,256]{2,0,1:T(4,128)(2,1)S(1)} fusion(f32[8,4,256]{2,1,0:T(4,128)} %shard_map.100), kind=kLoop, calls=%fused_computation | loop fusion | flops 8192 | bytes 49152 | tf_op jit(solution)/shard_map/convert_element_type | solution.py:447
  49.6 0.6 %convert_element_type.19 = bf16[1,8192]{1,0:T(2,128)(2,1)} reshape(bf16[4,8,256]{2,1,0:T(8,128)(2,1)S(1)} %copy.11) | data formatting | bytes 32768 | tf_op jit(solution)/shard_map/convert_element_type | solution.py:447
  (1 shorter events, 0.0 us)

commit v3 on v2

--- a/solution.py
+++ b/solution.py
@@ -28,6 +28,11 @@
 
 
 def each(count, step):
+    if count <= 32:
+        for d in range(1, count):
+            step(d)
+        return
+
     def one(i, carry):
         step(i + 1)
         return carry
@@ -35,54 +40,48 @@
     lax.fori_loop(0, count - 1, one, 0)
 
 
-def greet(segment):
+def greet(n):
+    me = lax.axis_index("seq")
+    sem = pltpu.get_barrier_semaphore()
+    each(n, lambda d: pl.semaphore_signal(sem, inc=1, device_id={"seq": lax.rem(me + d, n)}))
+
+
+def greeted(n):
+    pl.semaphore_wait(pltpu.get_barrier_semaphore(), n - 1)
+
+
+def exchange(ref, sems, segment, source=None, over="plane", rows=None):
     z, j = place(segment)
-    sem = pltpu.get_barrier_semaphore()
-
-    def plane(d):
-        to = z * segment + lax.rem(j + d, segment)
-        pl.semaphore_signal(sem, inc=1, device_id={"seq": to})
-
-    def column(d):
-        to = lax.rem(z + d, PROMPT_COUNT) * segment + j
-        pl.semaphore_signal(sem, inc=1, device_id={"seq": to})
-
-    each(segment, plane)
-    each(PROMPT_COUNT, column)
-
-
-def greeted(segment):
-    pl.semaphore_wait(pltpu.get_barrier_semaphore(), segment - 1 + PROMPT_COUNT - 1)
-
-
-def exchange(ref, send, recv, segment, source=None, in_plane=True, rows=None):
-    z, j = place(segment)
-    count, mine = (segment, j) if in_plane else (PROMPT_COUNT, z)
+    n = segment * PROMPT_COUNT
+    count, mine = {
+        "plane": (segment, j),
+        "column": (PROMPT_COUNT, z),
+        "all": (n, lax.axis_index("seq")),
+    }[over]
+    send, recv = sems.at[0], sems.at[1]
 
     def view(array, block):
         return array.at[block] if rows is None else array.at[block, :, rows]
 
-    def copy(d, block):
-        peer = lax.rem(mine + d, count)
-        to = z * segment + peer if in_plane else peer * segment + j
-        return pltpu.make_async_remote_copy(
-            src_ref=view(ref, mine) if source is None else view(source, peer),
-            dst_ref=view(ref, block),
-            send_sem=send.at[d],
-            recv_sem=recv.at[block],
-            device_id={"seq": to},
-        )
-
     def start():
-        each(count, lambda d: copy(d, mine).start())
-
-    def wait_recv():
-        each(count, lambda d: copy(d, lax.rem(mine + d, count)).wait_recv())
-
-    def wait_send():
-        each(count, lambda d: copy(d, mine).wait_send())
-
-    return start, wait_recv, wait_send
+        def copy(d):
+            peer = lax.rem(mine + d, count)
+            to = {"plane": z * segment + peer, "column": peer * segment + j, "all": peer}[over]
+            pltpu.make_async_remote_copy(
+                src_ref=view(ref, mine) if source is None else view(source, peer),
+                dst_ref=view(ref, mine),
+                send_sem=send,
+                recv_sem=recv,
+                device_id={"seq": to},
+            ).start()
+
+        each(count, copy)
+
+    def wait(sem):
+        whole = view(ref, pl.ds(0, count - 1))
+        pltpu.make_async_copy(whole, whole, sem).wait()
+
+    return start, lambda: wait(recv), lambda: wait(send)
 
 
 def lanes(shape):
@@ -97,12 +96,11 @@
     return out
 
 
-def own_suffix(length, q, keys_ref, values_ref, key_ref, value_ref):
+def own_suffix(heads, logs, length, q, keys_ref, values_ref, key_ref, value_ref):
     parts = []
-    logs = jnp.zeros((GROUP, 128), jnp.float32)
     slots = keys_ref.shape[0]
     live = lanes((GROUP, slots)) < length
-    for k in range(KEY_VALUE_HEADS):
+    for k in heads:
         cut = slice(k * HEAD_SIZE, (k + 1) * HEAD_SIZE)
         head = q[k * GROUP : (k + 1) * GROUP]
         scores = lax.dot_general(
@@ -188,15 +186,13 @@
     rows_all,
     rows_wide,
     panel,
-    panel_column,
-    panel_rows,
     local_sems,
     sems,
     chunk_sems,
 ):
     z, j = place(segment)
     n = segment * PROMPT_COUNT
-    greet(segment)
+    greet(n)
     loads = [
         pltpu.make_async_copy(src, dst, local_sems.at[i])
         for i, (src, dst) in enumerate(
@@ -232,32 +228,25 @@
             block = jnp.where((prompts[b] == z) & (ranks[b] == s), b, block)
         slot_block.append(block)
 
-    greeted(segment)
-    ask = exchange(q_column, sems.at[0], sems.at[1], segment, in_plane=False)
+    greeted(n)
+    ask = exchange(q_column, sems.at[0], segment, over="column")
     ask[0]()
     loads[0].wait()
     loads[1].wait()
-    part, own_logs = own_suffix(length_ref[0], q, own_keys, own_values, key_ref, value_ref)
-    suffix[z] = part
-    suffix_logs[z] = own_logs
+    halves = []
+    own_logs = jnp.zeros((GROUP, 128), jnp.float32)
+    own = (length_ref[0], q, own_keys, own_values, key_ref, value_ref)
+    half, own_logs = own_suffix(range(4), own_logs, *own)
+    halves.append(half)
     ask[1]()
     for s in range(SLOTS):
         q_all[j, s] = pick(slot_block[s], [q_column[b] for b in range(PROMPT_COUNT)])
 
     def ask_plane(i):
-        return exchange(
-            q_all, chunk_sems.at[0, i], chunk_sems.at[1, i], segment, rows=pair_rows(i)
-        )
+        return exchange(q_all, chunk_sems.at[0, i], segment, rows=pair_rows(i))
 
     def answer(i):
-        return exchange(
-            got,
-            chunk_sems.at[2, i],
-            chunk_sems.at[3, i],
-            segment,
-            source=parts,
-            rows=pair_rows(i),
-        )
+        return exchange(got, chunk_sems.at[1, i], segment, source=parts, rows=pair_rows(i))
 
     pairs = KEY_VALUE_HEADS // 2
 
@@ -269,8 +258,12 @@
         lax.fori_loop(0, pairs, one, 0)
 
     all_pairs(lambda i: ask_plane(i)[0]())
-    tell = exchange(suffix, sems.at[2], sems.at[3], segment, in_plane=False)
-    tell_logs = exchange(suffix_logs, sems.at[4], sems.at[5], segment, in_plane=False)
+    half, own_logs = own_suffix(range(4, KEY_VALUE_HEADS), own_logs, *own)
+    halves.append(half)
+    suffix[z] = jnp.concatenate(halves, axis=0)
+    suffix_logs[z] = own_logs
+    tell = exchange(suffix, sems.at[1], segment, over="column")
+    tell_logs = exchange(suffix_logs, sems.at[2], segment, over="column")
     tell[0]()
     tell_logs[0]()
     loads[2].wait()
@@ -282,7 +275,7 @@
         answer(i)[0]()
 
     all_pairs(work)
-    answer_logs = exchange(got_logs, sems.at[6], sems.at[7], segment, source=logs)
+    answer_logs = exchange(got_logs, sems.at[3], segment, source=logs)
     answer_logs[0]()
     got[j] = parts[j]
     got_logs[j] = logs[j]
@@ -302,8 +295,8 @@
                 w = spread(weights[i, s * GROUP : (s + 1) * GROUP], pair)
                 acc = acc + w * got[i, s, rows].astype(jnp.float32)
             column[z, s, rows] = acc.astype(jnp.bfloat16)
-    share = exchange(column, sems.at[8], sems.at[9], segment, in_plane=False)
-    share_logs = exchange(column_logs, sems.at[10], sems.at[11], segment, in_plane=False)
+    share = exchange(column, sems.at[4], segment, over="column")
+    share_logs = exchange(column_logs, sems.at[5], segment, over="column")
     share_logs[0]()
     share[0]()
     tell_logs[1]()
@@ -334,9 +327,13 @@
             row = spread(prompt_weight, pair) * prompt[rows]
             row = row + spread(own_weight, pair) * suffix[b, rows]
             rows_all[j, b, rows] = row.astype(jnp.bfloat16)
-    gather = exchange(rows_all, sems.at[12], sems.at[13], segment)
+    gather = exchange(rows_all, sems.at[6], segment)
     gather[0]()
     loads[4].wait()
+    for group in (ask, tell, tell_logs, answer_logs, share, share_logs):
+        group[2]()
+    all_pairs(lambda i: ask_plane(i)[2]())
+    all_pairs(lambda i: answer(i)[2]())
     gather[1]()
 
     def widen(i, carry):
@@ -360,22 +357,15 @@
     acc = lax.fori_loop(
         0, QUERY_HEADS // 8, project, jnp.zeros((n, weight.shape[1]), jnp.float32)
     )
-    panel[...] = acc.reshape(panel.shape)
-    back = exchange(panel_column, sems.at[14], sems.at[15], segment, source=panel, in_plane=False)
-    back[0]()
-    panel_column[z] = panel[z]
-    back[1]()
-    for i in range(segment):
-        for p in range(PROMPT_COUNT):
-            panel_rows[i, p : p + 1, :] = panel_column[p, i : i + 1, :]
-    home = exchange(out_ref, sems.at[16], sems.at[17], segment, source=panel_rows)
+    for r in range(n):
+        panel[r] = acc[r : r + 1]
+    home = exchange(out_ref, sems.at[7], segment, source=panel, over="all")
     home[0]()
-    out_ref[j] = panel_rows[j]
+    me = lax.axis_index("seq")
+    out_ref[me] = panel[me]
+    gather[2]()
     home[1]()
-    for group in (ask, tell, tell_logs, answer_logs, share, share_logs, gather, back, home):
-        group[2]()
-    all_pairs(lambda i: ask_plane(i)[2]())
-    all_pairs(lambda i: answer(i)[2]())
+    home[2]()
 
 
 def body(
@@ -397,11 +387,10 @@
     heads, size = QUERY_HEADS, HEAD_SIZE
     columns = out_weight.shape[1]
     bf, f32 = jnp.bfloat16, jnp.float32
-    most = max(segment, PROMPT_COUNT)
     own_keys, own_values = private_cached_keys[0], private_cached_values[0]
     out = pl.pallas_call(
         functools.partial(kernel, segment),
-        out_shape=jax.ShapeDtypeStruct((segment, PROMPT_COUNT, columns), f32),
+        out_shape=jax.ShapeDtypeStruct((n, 1, columns), f32),
         in_specs=[SMEM, SMEM] + [VMEM] * 3 + [ANY] * 5,
         out_specs=VMEM,
         scratch_shapes=[
@@ -422,12 +411,10 @@
             pltpu.VMEM((PROMPT_COUNT, SLOTS * GROUP, 128), f32),
             pltpu.VMEM((segment, PROMPT_COUNT, heads, size), bf),
             pltpu.VMEM((n * heads, size), f32),
-            pltpu.VMEM((PROMPT_COUNT, segment, columns), f32),
-            pltpu.VMEM((PROMPT_COUNT, segment, columns), f32),
-            pltpu.VMEM((segment, PROMPT_COUNT, columns), f32),
+            pltpu.VMEM((n, 1, columns), f32),
             pltpu.SemaphoreType.DMA((5,)),
-            pltpu.SemaphoreType.DMA((18, most)),
-            pltpu.SemaphoreType.DMA((4, KEY_VALUE_HEADS // 2, most)),
+            pltpu.SemaphoreType.DMA((8, 2)),
+            pltpu.SemaphoreType.DMA((2, KEY_VALUE_HEADS // 2, 2)),
         ],
         compiler_params=pltpu.CompilerParams(
             collective_id=0, has_side_effects=True, vmem_limit_bytes=56 << 20
@@ -444,7 +431,7 @@
         shared_prompt_values,
         out_weight,
     )
-    return out.transpose(1, 0, 2).reshape(1, width).astype(bf)
+    return out.reshape(1, width).astype(bf)
 
 
 def solution(mesh):

time: 50.5 us -> 45.3 us (0.90)
  Pallas kernels: 48.2 us -> 43 us
  local copies, waits for them, and re-layouts: 0.64 us -> 0 us
  other arithmetic: 0.77 us -> 1.4 us
    pallas_call x1, Pallas kernels: 48.2 us -> 43 us  [body(): pl.pallas_call(functools.partial(kernel, segment), out_shape=jax.ShapeDty...]
    convert_element_type x2 -> x0, local copies, waits for them, and re-layouts: 0.64 us -> none  [body(): return out.transpose(1, 0, 2).reshape(1, width).astype(bf)]
    convert_element_type x1, other arithmetic: 0.77 us -> 1.4 us  [body(): return out.reshape(1, width).astype(bf)]
where the time goes in v3:
time: 45.3 us; the launch traced here: 45.1 us
  Pallas kernels  43 us (95%)
  other arithmetic  1.4 us (3%)
  between operations  0.66 us (1%)
    pallas_call x1, Pallas kernels, body(): pl.pallas_call(functools.partial(kernel, segment), out_shape=jax.ShapeDty...  43 us
    convert_element_type x1, other arithmetic, body(): return out.reshape(1, width).astype(bf)  1.4 us

profile of v3, /device:TPU:0, one launch (start us, length us, event | category | flops | bytes accessed | tf_op | source)
XLA Modules:
  0.0 45.1 jit_solution(7790302569154857292)
XLA Ops:
  0.7 43.0 %shard_map.100 = f32[32,1,256]{2,1,0:T(1,128)} custom-call(s32[4]{0:T(128)} %prompts_ref.1, s32[1]{0:T(128)S(6)} %copy.11.length_ref, bf16[1,8192]{1,0:T(2,128)(2,1)} %q_ref.1, bf16[1,1024]{1,0:T(2,128)(2,1)} %key_ref.1, bf16[1,1024]{1,0:T(2,128)(2,1)} %value_ref.1, bf16[256,1024]{1,0:T(8,128)(2,1)} %bitcast.3, bf16[256,1024]{1,0:T(8,128)(2,1)} %bitcast.4, ...), custom_call_target="tpu_custom_call" | custom-call | tf_op jit(solution)/shard_map/pallas_call | solution.py:391
  43.7 1.4 %convert_element_type.14 = bf16[32,1,256]{2,1,0:T(2,128)(2,1)} convert(f32[32,1,256]{2,1,0:T(1,128)} %shard_map.100) | non-fusion elementwise | flops 8192 | bytes 49152 | tf_op jit(solution)/shard_map/convert_element_type | solution.py:434

commit v4 on v3

--- a/solution.py
+++ b/solution.py
@@ -14,6 +14,7 @@
 HEAD_SIZE = 128
 PROMPT_COUNT = 4
 SLOTS = 2
+HALF_HEADS = QUERY_HEADS // 2
 SCALE = 1.0 / math.sqrt(HEAD_SIZE)
 SCALE_LOG2 = SCALE * math.log2(math.e)
 VMEM = pl.BlockSpec(memory_space=pltpu.VMEM)
@@ -129,7 +130,7 @@
 
 
 def pair_rows(i):
-    return pl.ds(pl.multiple_of(i * 16, 16), 16)
+    return pl.ds(i * 16, 16)
 
 
 def attend(i, segment, q_ref, keys_ref, values_ref, part_ref, logs_ref):
@@ -139,7 +140,7 @@
     parts = []
     logs = logs_ref[...].reshape(rows, 128)
     for h in range(2):
-        cut = pl.ds(pl.multiple_of((i * 2 + h) * HEAD_SIZE, HEAD_SIZE), HEAD_SIZE)
+        cut = pl.ds((i * 2 + h) * HEAD_SIZE, HEAD_SIZE)
         head = q[:, h].reshape(rows, HEAD_SIZE).astype(jnp.bfloat16)
         scores = lax.dot_general(head, keys_ref[:, cut], NT, preferred_element_type=jnp.float32)
         top = jnp.max(scores, axis=1, keepdims=True)
@@ -236,8 +237,8 @@
     halves = []
     own_logs = jnp.zeros((GROUP, 128), jnp.float32)
     own = (length_ref[0], q, own_keys, own_values, key_ref, value_ref)
-    half, own_logs = own_suffix(range(4), own_logs, *own)
-    halves.append(half)
+    part, own_logs = own_suffix(range(4), own_logs, *own)
+    halves.append(part)
     ask[1]()
     for s in range(SLOTS):
         q_all[j, s] = pick(slot_block[s], [q_column[b] for b in range(PROMPT_COUNT)])
@@ -249,17 +250,27 @@
         return exchange(got, chunk_sems.at[1, i], segment, source=parts, rows=pair_rows(i))
 
     pairs = KEY_VALUE_HEADS // 2
-
-    def all_pairs(step):
-        def one(i, carry):
-            step(i)
-            return carry
-
-        lax.fori_loop(0, pairs, one, 0)
-
-    all_pairs(lambda i: ask_plane(i)[0]())
-    half, own_logs = own_suffix(range(4, KEY_VALUE_HEADS), own_logs, *own)
-    halves.append(half)
+    half = pairs // 2
+
+    def head_rows(c):
+        return pl.ds(c * HALF_HEADS, HALF_HEADS)
+
+    def answer_logs(c):
+        return exchange(got_logs.at[c], sems.at[3 + c], segment, source=logs.at[c])
+
+    def share(c):
+        return exchange(column, sems.at[5 + c], segment, over="column", rows=head_rows(c))
+
+    def share_logs(c):
+        return exchange(column_logs.at[c], sems.at[7 + c], segment, over="column")
+
+    def gather(c):
+        return exchange(rows_all, sems.at[9 + c], segment, rows=head_rows(c))
+
+    for i in range(pairs):
+        ask_plane(i)[0]()
+    part, own_logs = own_suffix(range(4, KEY_VALUE_HEADS), own_logs, *own)
+    halves.append(part)
     suffix[z] = jnp.concatenate(halves, axis=0)
     suffix_logs[z] = own_logs
     tell = exchange(suffix, sems.at[1], segment, over="column")
@@ -270,100 +281,118 @@
     loads[3].wait()
 
     def work(i):
+        c = i // half
         ask_plane(i)[1]()
-        attend(i, segment, q_all, keys, values, parts, logs)
+        attend(i, segment, q_all, keys, values, parts, logs.at[c])
         answer(i)[0]()
-
-    all_pairs(work)
-    answer_logs = exchange(got_logs, sems.at[3], segment, source=logs)
-    answer_logs[0]()
-    got[j] = parts[j]
-    got_logs[j] = logs[j]
-    answer_logs[1]()
-    all_logs = got_logs[...]
-    best = jnp.max(all_logs, axis=0)
-    weights = jnp.exp(all_logs - best[None])
-    total = jnp.sum(weights, axis=0)
-    weights = weights / total[None]
-    column_logs[z] = best + jnp.log(total)
-    all_pairs(lambda i: answer(i)[1]())
-    for s in range(SLOTS):
-        for pair in range(pairs):
-            rows = slice(pair * 16, pair * 16 + 16)
-            acc = jnp.zeros((16, HEAD_SIZE), jnp.float32)
-            for i in range(segment):
-                w = spread(weights[i, s * GROUP : (s + 1) * GROUP], pair)
-                acc = acc + w * got[i, s, rows].astype(jnp.float32)
-            column[z, s, rows] = acc.astype(jnp.bfloat16)
-    share = exchange(column, sems.at[4], segment, over="column")
-    share_logs = exchange(column_logs, sems.at[5], segment, over="column")
-    share_logs[0]()
-    share[0]()
+        if i % half == half - 1:
+            answer_logs(c)[0]()
+            got_logs[c, j] = logs[c, j]
+        got[j, :, pair_rows(i), :] = parts[j, :, pair_rows(i), :]
+
+    def combine(c):
+        answer_logs(c)[1]()
+        all_logs = got_logs[c]
+        best = jnp.max(all_logs, axis=0)
+        weights = jnp.exp(all_logs - best[None])
+        total = jnp.sum(weights, axis=0)
+        weights = weights / total[None]
+        column_logs[c, z] = best + jnp.log(total)
+        share_logs(c)[0]()
+        for pair in range(c * half, (c + 1) * half):
+            answer(pair)[1]()
+            for s in range(SLOTS):
+                rows = slice(pair * 16, pair * 16 + 16)
+                acc = jnp.zeros((16, HEAD_SIZE), jnp.float32)
+                for i in range(segment):
+                    w = spread(weights[i, s * GROUP : (s + 1) * GROUP], pair)
+                    acc = acc + w * got[i, s, rows].astype(jnp.float32)
+                column[z, s, rows] = acc.astype(jnp.bfloat16)
+        share(c)[0]()
+
+    def finish_rows(c):
+        share_logs(c)[1]()
+        share(c)[1]()
+        for b in range(PROMPT_COUNT):
+            at = prompts[b] * SLOTS + ranks[b]
+            prompt_logs = pick(
+                at,
+                [
+                    column_logs[c, p, s * GROUP : (s + 1) * GROUP]
+                    for p in range(PROMPT_COUNT)
+                    for s in range(SLOTS)
+                ],
+            )
+            own_logs = suffix_logs[b]
+            best = jnp.maximum(prompt_logs, own_logs)
+            prompt_weight = jnp.exp(prompt_logs - best)
+            own_weight = jnp.exp(own_logs - best)
+            total = prompt_weight + own_weight
+            prompt_weight = prompt_weight / total
+            own_weight = own_weight / total
+            for pair in range(c * half, (c + 1) * half):
+                rows = slice(pair * 16, pair * 16 + 16)
+                prompt = pick(
+                    at, [column[i // SLOTS, i % SLOTS, rows] for i in range(PROMPT_COUNT * SLOTS)]
+                )
+                row = spread(prompt_weight, pair) * prompt.astype(jnp.float32)
+                row = row + spread(own_weight, pair) * suffix[b, rows]
+                rows_all[j, b, rows] = row.astype(jnp.bfloat16)
+        gather(c)[0]()
+
+    def project(c, acc):
+        gather(c)[1]()
+
+        def widen(i, carry):
+            for b in range(PROMPT_COUNT):
+                at = (b * segment + i) * QUERY_HEADS + c * HALF_HEADS
+                rows_wide[pl.ds(pl.multiple_of(at, HALF_HEADS), HALF_HEADS), :] = rows_all[
+                    i, b, head_rows(c), :
+                ].astype(jnp.float32)
+            return carry
+
+        lax.fori_loop(0, segment, widen, 0)
+
+        def some(i, acc):
+            for pair in range(4):
+                h = i * 8 + pair * 2
+                both = [rows_wide[pl.ds(h + o, n, stride=QUERY_HEADS), :] for o in range(2)]
+                left = jnp.concatenate(both, axis=1).astype(jnp.bfloat16)
+                at = pl.multiple_of(h * HEAD_SIZE, 2 * HEAD_SIZE)
+                right = weight[pl.ds(at, 2 * HEAD_SIZE), :]
+                acc = acc + jnp.dot(left, right, preferred_element_type=jnp.float32)
+            return acc
+
+        return lax.fori_loop(c * HALF_HEADS // 8, (c + 1) * HALF_HEADS // 8, some, acc)
+
+    work(0)
+    work(1)
+    work(2)
+    combine(0)
+    work(3)
     tell_logs[1]()
     tell[1]()
-    share_logs[1]()
-    share[1]()
-    for b in range(PROMPT_COUNT):
-        at = prompts[b] * SLOTS + ranks[b]
-        prompt = pick(at, [column[i // SLOTS, i % SLOTS] for i in range(PROMPT_COUNT * SLOTS)])
-        prompt = prompt.astype(jnp.float32)
-        prompt_logs = pick(
-            at,
-            [
-                column_logs[p, s * GROUP : (s + 1) * GROUP]
-                for p in range(PROMPT_COUNT)
-                for s in range(SLOTS)
-            ],
-        )
-        own_logs = suffix_logs[b]
-        best = jnp.maximum(prompt_logs, own_logs)
-        prompt_weight = jnp.exp(prompt_logs - best)
-        own_weight = jnp.exp(own_logs - best)
-        total = prompt_weight + own_weight
-        prompt_weight = prompt_weight / total
-        own_weight = own_weight / total
-        for pair in range(pairs):
-            rows = slice(pair * 16, pair * 16 + 16)
-            row = spread(prompt_weight, pair) * prompt[rows]
-            row = row + spread(own_weight, pair) * suffix[b, rows]
-            rows_all[j, b, rows] = row.astype(jnp.bfloat16)
-    gather = exchange(rows_all, sems.at[6], segment)
-    gather[0]()
+    finish_rows(0)
+    combine(1)
     loads[4].wait()
-    for group in (ask, tell, tell_logs, answer_logs, share, share_logs):
+    for group in (ask, tell, tell_logs, answer_logs(0), answer_logs(1), share_logs(0), share(0)):
         group[2]()
-    all_pairs(lambda i: ask_plane(i)[2]())
-    all_pairs(lambda i: answer(i)[2]())
-    gather[1]()
-
-    def widen(i, carry):
-        for b in range(PROMPT_COUNT):
-            at = pl.multiple_of((b * segment + i) * QUERY_HEADS, QUERY_HEADS)
-            rows_wide[pl.ds(at, QUERY_HEADS), :] = rows_all[i, b].astype(jnp.float32)
-        return carry
-
-    lax.fori_loop(0, segment, widen, 0)
-
-    def project(i, acc):
-        for pair in range(4):
-            h = i * 8 + pair * 2
-            both = [rows_wide[pl.ds(h + o, n, stride=QUERY_HEADS), :] for o in range(2)]
-            left = jnp.concatenate(both, axis=1).astype(jnp.bfloat16)
-            at = pl.multiple_of(h * HEAD_SIZE, 2 * HEAD_SIZE)
-            right = weight[pl.ds(at, 2 * HEAD_SIZE), :]
-            acc = acc + jnp.dot(left, right, preferred_element_type=jnp.float32)
-        return acc
-
-    acc = lax.fori_loop(
-        0, QUERY_HEADS // 8, project, jnp.zeros((n, weight.shape[1]), jnp.float32)
-    )
+    for i in range(pairs):
+        ask_plane(i)[2]()
+        answer(i)[2]()
+    acc = project(0, jnp.zeros((n, weight.shape[1]), jnp.float32))
+    finish_rows(1)
+    share_logs(1)[2]()
+    share(1)[2]()
+    acc = project(1, acc)
     for r in range(n):
         panel[r] = acc[r : r + 1]
-    home = exchange(out_ref, sems.at[7], segment, source=panel, over="all")
+    home = exchange(out_ref, sems.at[11], segment, source=panel, over="all")
     home[0]()
     me = lax.axis_index("seq")
     out_ref[me] = panel[me]
-    gather[2]()
+    gather(0)[2]()
+    gather(1)[2]()
     home[1]()
     home[2]()
 
@@ -404,16 +433,16 @@
             pltpu.VMEM((PROMPT_COUNT, heads, size), f32),
             pltpu.VMEM((PROMPT_COUNT, GROUP, 128), f32),
             pltpu.VMEM((segment, SLOTS, heads, size), bf),
-            pltpu.VMEM((segment, SLOTS * GROUP, 128), f32),
+            pltpu.VMEM((2, segment, SLOTS * GROUP, 128), f32),
             pltpu.VMEM((segment, SLOTS, heads, size), bf),
-            pltpu.VMEM((segment, SLOTS * GROUP, 128), f32),
+            pltpu.VMEM((2, segment, SLOTS * GROUP, 128), f32),
             pltpu.VMEM((PROMPT_COUNT, SLOTS, heads, size), bf),
-            pltpu.VMEM((PROMPT_COUNT, SLOTS * GROUP, 128), f32),
+            pltpu.VMEM((2, PROMPT_COUNT, SLOTS * GROUP, 128), f32),
             pltpu.VMEM((segment, PROMPT_COUNT, heads, size), bf),
             pltpu.VMEM((n * heads, size), f32),
             pltpu.VMEM((n, 1, columns), f32),
             pltpu.SemaphoreType.DMA((5,)),
-            pltpu.SemaphoreType.DMA((8, 2)),
+            pltpu.SemaphoreType.DMA((12, 2)),
             pltpu.SemaphoreType.DMA((2, KEY_VALUE_HEADS // 2, 2)),
         ],
         compiler_params=pltpu.CompilerParams(

time: 45.3 us -> 43.6 us (0.962)
  Pallas kernels: 43 us -> 41.3 us
    pallas_call x1, Pallas kernels: 43 us -> 41.3 us  [body(): pl.pallas_call(functools.partial(kernel, segment), out_shape=jax.ShapeDty...]
where the time goes in v4:
time: 43.6 us; the launch traced here: 43.4 us
  Pallas kernels  41.3 us (95%)
  other arithmetic  1.4 us (3%)
  between operations  0.66 us (2%)
    pallas_call x1, Pallas kernels, body(): pl.pallas_call(functools.partial(kernel, segment), out_shape=jax.ShapeDty...  41.3 us
    convert_element_type x1, other arithmetic, body(): return out.reshape(1, width).astype(bf)  1.4 us

profile of v4, /device:TPU:0, one launch (start us, length us, event | category | flops | bytes accessed | tf_op | source)
XLA Modules:
  0.0 43.4 jit_solution(13795807478318282836)
XLA Ops:
  0.7 41.3 %shard_map.100 = f32[32,1,256]{2,1,0:T(1,128)} custom-call(s32[4]{0:T(128)} %prompts_ref.1, s32[1]{0:T(128)S(6)} %copy.11.length_ref, bf16[1,8192]{1,0:T(2,128)(2,1)} %q_ref.1, bf16[1,1024]{1,0:T(2,128)(2,1)} %key_ref.1, bf16[1,1024]{1,0:T(2,128)(2,1)} %value_ref.1, bf16[256,1024]{1,0:T(8,128)(2,1)} %bitcast.3, bf16[256,1024]{1,0:T(8,128)(2,1)} %bitcast.4, ...), custom_call_target="tpu_custom_call" | custom-call | tf_op jit(solution)/shard_map/pallas_call | solution.py:420
  42.0 1.4 %convert_element_type.14 = bf16[32,1,256]{2,1,0:T(2,128)(2,1)} convert(f32[32,1,256]{2,1,0:T(1,128)} %shard_map.100) | non-fusion elementwise | flops 8192 | bytes 49152 | tf_op jit(solution)/shard_map/convert_element_type | solution.py:463

commit v5 on v4

--- a/solution.py
+++ b/solution.py
@@ -380,8 +380,8 @@
     for i in range(pairs):
         ask_plane(i)[2]()
         answer(i)[2]()
+    finish_rows(1)
     acc = project(0, jnp.zeros((n, weight.shape[1]), jnp.float32))
-    finish_rows(1)
     share_logs(1)[2]()
     share(1)[2]()
     acc = project(1, acc)

time: 43.6 us -> 42.7 us (0.979)
  Pallas kernels: 41.3 us -> 40.4 us
    pallas_call x1, Pallas kernels: 41.3 us -> 40.4 us  [body(): pl.pallas_call(functools.partial(kernel, segment), out_shape=jax.ShapeDty...]
where the time goes in v5:
time: 42.7 us; the launch traced here: 42.5 us
  Pallas kernels  40.4 us (95%)
  other arithmetic  1.4 us (3%)
  between operations  0.66 us (2%)
    pallas_call x1, Pallas kernels, body(): pl.pallas_call(functools.partial(kernel, segment), out_shape=jax.ShapeDty...  40.4 us
    convert_element_type x1, other arithmetic, body(): return out.reshape(1, width).astype(bf)  1.4 us

profile of v5, /device:TPU:0, one launch (start us, length us, event | category | flops | bytes accessed | tf_op | source)
XLA Modules:
  0.0 42.5 jit_solution(6680091890045750837)
XLA Ops:
  0.7 40.4 %shard_map.100 = f32[32,1,256]{2,1,0:T(1,128)} custom-call(s32[4]{0:T(128)} %prompts_ref.1, s32[1]{0:T(128)S(6)} %copy.11.length_ref, bf16[1,8192]{1,0:T(2,128)(2,1)} %q_ref.1, bf16[1,1024]{1,0:T(2,128)(2,1)} %key_ref.1, bf16[1,1024]{1,0:T(2,128)(2,1)} %value_ref.1, bf16[256,1024]{1,0:T(8,128)(2,1)} %bitcast.3, bf16[256,1024]{1,0:T(8,128)(2,1)} %bitcast.4, ...), custom_call_target="tpu_custom_call" | custom-call | tf_op jit(solution)/shard_map/pallas_call | solution.py:420
  41.1 1.4 %convert_element_type.14 = bf16[32,1,256]{2,1,0:T(2,128)(2,1)} convert(f32[32,1,256]{2,1,0:T(1,128)} %shard_map.100) | non-fusion elementwise | flops 8192 | bytes 49152 | tf_op jit(solution)/shard_map/convert_element_type | solution.py:463
